TPU v7x, 32 devices: a whole 2x2x4 slice. The times are simulated.
32 devices in a mesh: dp: 4 (over y, core), mp: 8 (over z, x).
Axes of the slice: x: 2, y: 2, z: 4, core: 2. Of those that a mesh axis runs over, the one named last changes fastest.
Arguments:
- inputs: bfloat16 [32768, 768], P(('dp', 'mp')), may hold values from -6 to 6
- segments: int32 [32, 1024], P('dp'), may hold values from 0 to 3, never falling along the last dimension, each value on 1 to 384 neighbouring positions
- ln1_gain: float32 [768], replicated, may hold values from 0.1 to 1.9
- ln1_bias: float32 [768], replicated, may hold values from -3 to 3
- w_query: bfloat16 [768, 768], P(None, 'mp'), may hold values from -0.3125 to 0.3125
- w_key: bfloat16 [768, 768], P(None, 'mp'), may hold values from -0.21875 to 0.21875
- w_value: bfloat16 [768, 768], P(None, 'mp'), may hold values from -0.21875 to 0.21875
- w_output: bfloat16 [768, 768], P('mp'), may hold values from -3.5 to 3.5
- ln2_gain: float32 [768], replicated, may hold values from 0.1 to 1.9
- ln2_bias: float32 [768], replicated, may hold values from -3 to 3
- w_up: bfloat16 [768, 3072], P(None, 'mp'), may hold values from -0.21875 to 0.21875
- w_down: bfloat16 [3072, 768], P('mp'), may hold values from -0.109375 to 0.109375
- cotangent: bfloat16 [32768, 768], P(('dp', 'mp')), may hold values from -6 to 6
Outputs:
- output: bfloat16 [32768, 768], P(('dp', 'mp'))
- in_grad: bfloat16 [32768, 768], P(('dp', 'mp'))
- grad_ln1_gain: float32 [768], P('mp')
- grad_ln1_bias: float32 [768], P('mp')
- grad_w_query: float32 [768, 768], P(None, 'mp')
- grad_w_key: float32 [768, 768], P(None, 'mp')
- grad_w_value: float32 [768, 768], P(None, 'mp')
- grad_w_output: float32 [768, 768], P('mp')
- grad_ln2_gain: float32 [768], P('mp')
- grad_ln2_bias: float32 [768], P('mp')
- grad_w_up: float32 [768, 3072], P(None, 'mp')
- grad_w_down: float32 [3072, 768], P('mp')
Inputs may be any that keep to these rules, and one draw needn't show every extreme that they name: `segments`: within each sequence the image numbers never fall, every image 0 to 3 holds 1 to 384 tokens, and one image of each sequence holds exactly 384.
All inputs are finite; a program needn't handle non-finite values.
Results may differ from a plain program's by a relative error of at most 0.012.
The roundings to bfloat16 on the way count: a program that leaves them out, or rounds other values in their place, can miss the bound.
Values may be sent and summed in bfloat16 or wider, within the bound.
No kernel may reach another device: no remote copies, remote signals or barrier semaphores. Data moves between devices by JAX's collectives and lax.ppermute only.
A program may use at most 256 MiB of HBM per device.

v0:
```python
import functools
import math

import jax
import jax.numpy as jnp
from jax import lax
from jax.experimental import pallas as pl
from jax.experimental.pallas import tpu as pltpu
from jax.sharding import PartitionSpec as P

HEAD_DIM = 48
PAIR = 2 * HEAD_DIM
IMAGES = 4
TILE = 128
norm_eps = 1e-06
negative_fill = -1e30
SCALE = HEAD_DIM ** (-0.5)
SCALE_LOG2 = SCALE * math.log2(math.e)
BF16 = jnp.bfloat16
F32 = jnp.float32


def layer_norm(values, gain, bias):
    center = jnp.mean(values, axis=-1, keepdims=True)
    shifted = values - center
    spread = jnp.mean(shifted * shifted, axis=-1, keepdims=True)
    return shifted * lax.rsqrt(spread + norm_eps) * gain + bias


def layer_norm_back(values, gain, grad):
    shifted = values - jnp.mean(values, axis=-1, keepdims=True)
    scale = lax.rsqrt(jnp.mean(shifted * shifted, axis=-1, keepdims=True) + norm_eps)
    unit = shifted * scale
    scaled = grad * gain
    back = scale * (
        scaled
        - jnp.mean(scaled, axis=-1, keepdims=True)
        - unit * jnp.mean(scaled * unit, axis=-1, keepdims=True)
    )
    return back, jnp.sum(grad * unit, axis=0, keepdims=True), jnp.sum(grad, axis=0, keepdims=True)


def dot(left, right, dims):
    return lax.dot_general(left, right, (dims, ((), ())), preferred_element_type=F32)


NN = ((1,), (0,))
NT = ((1,), (1,))
TN = ((0,), (0,))


def window_kinds(tiles):
    return tuple(n for n in (2, 3, 4, 5, 6, 7) if n < tiles) + (tiles,)


def image_rows(segs, length):
    row = lax.broadcasted_iota(jnp.int32, (TILE - PAIR, length), 0)
    here = row == segs
    one_hot = jnp.where(here, 1.0, 0.0).astype(BF16)
    fill = jnp.where(jnp.logical_or(here, row >= IMAGES), 0.0, negative_fill).astype(BF16)
    return one_hot, fill


def side_by_side(pair, extra):
    blank = jnp.zeros((HEAD_DIM, TILE), BF16)
    left = jnp.concatenate([pair[:HEAD_DIM], blank, extra], axis=0)
    right = jnp.concatenate([blank, pair[HEAD_DIM:], extra], axis=0)
    return jnp.concatenate([left, right], axis=1)


def pair_places(ref):
    cores, count = ref.shape[0], ref.shape[1]
    return [(core, top) for core in range(cores) for top in range(0, count, PAIR)]


def attend_forward_kernel(
    first_ref, kind_ref, flip_ref, segs_ref, qv_ref, k_ref, out_ref, lse_ref, hot_ref, keys_ref, vals_ref
):
    length = k_ref.shape[-1]
    at_q = flip_ref[0]
    places = pair_places(k_ref)
    one_hot, fill = image_rows(segs_ref[...], length)
    hot_ref[...] = one_hot
    for j, (core, top) in enumerate(places):
        rows = slice(top, top + PAIR)
        keys_ref[j] = jnp.concatenate([k_ref[core, rows, :], fill], axis=0).T
        vals_ref[j] = jnp.concatenate(
            [qv_ref[core, 1 - at_q, rows, :], jnp.ones((16, length), BF16)], axis=0
        )

    def block(b, carry):
        at = pl.ds(pl.multiple_of(b * TILE, TILE), TILE)
        first = pl.multiple_of(first_ref[b] * TILE, TILE)

        def variant(tiles):
            span = pl.ds(first, tiles * TILE)
            scores = [
                dot(
                    keys_ref[j, span, :],
                    side_by_side(qv_ref[core, at_q, top : top + PAIR, at], hot_ref[:, at]),
                    NN,
                )
                for j, (core, top) in enumerate(places)
            ]
            for j, (core, top) in enumerate(places):
                most = jnp.max(scores[j], axis=0, keepdims=True)
                expo = jnp.exp2((scores[j] - most) * SCALE_LOG2).astype(BF16)
                mixed = dot(vals_ref[j, :, span], expo, NN)
                total = mixed[PAIR : PAIR + 1, :]
                inverse = 1.0 / total
                out_ref[core, top : top + HEAD_DIM, at] = (
                    mixed[:HEAD_DIM, :TILE] * inverse[:, :TILE]
                ).astype(BF16)
                out_ref[core, top + HEAD_DIM : top + PAIR, at] = (
                    mixed[HEAD_DIM:PAIR, TILE:] * inverse[:, TILE:]
                ).astype(BF16)
                lse_ref[j, pl.ds(b, 1), :] = most * SCALE_LOG2 + jnp.log2(total)

        for tiles in window_kinds(length // TILE):
            pl.when(kind_ref[b] == tiles)(functools.partial(variant, tiles))
        return carry

    lax.fori_loop(0, length // TILE, block, 0)


def attend_backward_kernel(
    first_ref,
    kind_ref,
    flip_ref,
    segs_ref,
    qv_ref,
    k_ref,
    att_ref,
    grad_ref,
    lse_ref,
    dqv_ref,
    dk_ref,
    hot_ref,
    keys_ref,
    vals_ref,
    queries_ref,
    grads_ref,
    key_sum_ref,
    val_sum_ref,
):
    length = k_ref.shape[-1]
    at_q = flip_ref[0]
    places = pair_places(k_ref)
    one_hot, fill = image_rows(segs_ref[...], length)
    hot_ref[...] = one_hot
    pad = jnp.zeros((TILE - PAIR, length), BF16)
    for j, (core, top) in enumerate(places):
        rows = slice(top, top + PAIR)
        keys_ref[j] = jnp.concatenate([k_ref[core, rows, :], fill], axis=0).T
        vals_ref[j] = jnp.concatenate([qv_ref[core, 1 - at_q, rows, :], pad], axis=0).T
        queries_ref[j] = jnp.concatenate([qv_ref[core, at_q, rows, :], pad], axis=0).T
        grads_ref[j] = jnp.concatenate([grad_ref[core, rows, :], pad], axis=0).T
    key_sum_ref[...] = jnp.zeros(key_sum_ref.shape, F32)
    val_sum_ref[...] = jnp.zeros(val_sum_ref.shape, F32)
    no_rows = jnp.zeros((TILE - PAIR, TILE), BF16)
    lane = lax.broadcasted_iota(jnp.int32, (TILE, TILE), 1)
    in_first = lane < HEAD_DIM

    def stacked(both):
        blank = jnp.zeros_like(both)
        return jnp.concatenate(
            [jnp.where(in_first, both, blank), jnp.where(in_first, blank, both)], axis=0
        )

    def block(b, carry):
        at = pl.ds(pl.multiple_of(b * TILE, TILE), TILE)
        first = pl.multiple_of(first_ref[b] * TILE, TILE)

        def variant(tiles):
            span = pl.ds(first, tiles * TILE)
            scores = [
                dot(
                    keys_ref[j, span, :],
                    side_by_side(qv_ref[core, at_q, top : top + PAIR, at], hot_ref[:, at]),
                    NN,
                )
                for j, (core, top) in enumerate(places)
            ]
            prob_grads = [
                dot(
                    vals_ref[j, span, :],
                    side_by_side(grad_ref[core, top : top + PAIR, at], no_rows),
                    NN,
                )
                for j, (core, top) in enumerate(places)
            ]
            for j, (core, top) in enumerate(places):
                rows = slice(top, top + PAIR)
                agree = grad_ref[core, rows, at].astype(F32) * att_ref[core, rows, at].astype(F32)
                delta = jnp.concatenate(
                    [
                        jnp.sum(agree[:HEAD_DIM], axis=0, keepdims=True),
                        jnp.sum(agree[HEAD_DIM:], axis=0, keepdims=True),
                    ],
                    axis=1,
                )
                probs = jnp.exp2(scores[j] * SCALE_LOG2 - lse_ref[j, pl.ds(b, 1), :])
                score_grad = (probs * (prob_grads[j] - delta)).astype(BF16)
                val_sum_ref[j, span, :] += dot(
                    probs.astype(BF16), stacked(grads_ref[j, at, :]), NN
                )
                key_sum_ref[j, span, :] += dot(score_grad, stacked(queries_ref[j, at, :]), NN)
                query_grad = dot(k_ref[core, rows, span], score_grad, NN) * SCALE
                dqv_ref[core, at_q, top : top + HEAD_DIM, at] = query_grad[
                    :HEAD_DIM, :TILE
                ].astype(BF16)
                dqv_ref[core, at_q, top + HEAD_DIM : top + PAIR, at] = query_grad[
                    HEAD_DIM:, TILE:
                ].astype(BF16)

        for tiles in window_kinds(length // TILE):
            pl.when(kind_ref[b] == tiles)(functools.partial(variant, tiles))
        return carry

    lax.fori_loop(0, length // TILE, block, 0)
    for j, (core, top) in enumerate(places):
        rows = slice(top, top + PAIR)
        dk_ref[core, rows, :] = (key_sum_ref[j] * SCALE).T[:PAIR].astype(BF16)
        dqv_ref[core, 1 - at_q, rows, :] = val_sum_ref[j].T[:PAIR].astype(BF16)


def windows(segs):
    length = segs.shape[0]
    tiles = length // TILE
    by_tile = segs.reshape(tiles, TILE)
    begin = jnp.sum(segs[None, :] < by_tile[:, :1], axis=1)
    end = jnp.sum(segs[None, :] <= by_tile[:, -1:], axis=1)
    first = begin // TILE
    need = (end + TILE - 1) // TILE - first
    kinds = jnp.asarray(window_kinds(tiles), jnp.int32)
    kind = jnp.min(jnp.where(kinds[None, :] >= need[:, None], kinds[None, :], tiles), axis=1)
    return jnp.minimum(first, tiles - kind).astype(jnp.int32), kind.astype(jnp.int32)


def attention_specs(keys):
    cores, count, length = keys.shape
    pairs = cores * count // PAIR
    step = pairs if pairs <= 4 else 4
    part = count * step // pairs
    rows = pl.BlockSpec((cores, part, length), lambda i, *_: (0, i, 0))
    two = pl.BlockSpec((cores, 2, part, length), lambda i, *_: (0, 0, i, 0))
    segs = pl.BlockSpec((1, length), lambda i, *_: (0, 0))
    lse = pl.BlockSpec((step, length // TILE, 2 * TILE), lambda i, *_: (i, 0, 0))
    return pairs, step, rows, two, segs, lse


def attend_forward(query_value, keys, place):
    first, kind, flip, segs = place
    length = segs.shape[0]
    pairs, step, rows, two, segs_spec, lse = attention_specs(keys)
    return pl.pallas_call(
        attend_forward_kernel,
        grid_spec=pltpu.PrefetchScalarGridSpec(
            num_scalar_prefetch=3,
            grid=(pairs // step,),
            in_specs=[segs_spec, two, rows],
            out_specs=[rows, lse],
            scratch_shapes=[
                pltpu.VMEM((TILE - PAIR, length), BF16),
                pltpu.VMEM((step, length, TILE), BF16),
                pltpu.VMEM((step, PAIR + 16, length), BF16),
            ],
        ),
        out_shape=[
            jax.ShapeDtypeStruct(keys.shape, BF16),
            jax.ShapeDtypeStruct((pairs, length // TILE, 2 * TILE), F32),
        ],
        compiler_params=pltpu.CompilerParams(vmem_limit_bytes=40 << 20),
        name="attend_forward",
    )(first, kind, flip, segs[None, :], query_value, keys)


def attend_backward(query_value, keys, attended, grad, lse, place):
    first, kind, flip, segs = place
    length = segs.shape[0]
    pairs, step, rows, two, segs_spec, lse_spec = attention_specs(keys)
    wide = pltpu.VMEM((step, length, TILE), BF16)
    total = pltpu.VMEM((step, length, TILE), F32)
    return pl.pallas_call(
        attend_backward_kernel,
        grid_spec=pltpu.PrefetchScalarGridSpec(
            num_scalar_prefetch=3,
            grid=(pairs // step,),
            in_specs=[segs_spec, two, rows, rows, rows, lse_spec],
            out_specs=[two, rows],
            scratch_shapes=[
                pltpu.VMEM((TILE - PAIR, length), BF16),
                wide,
                wide,
                wide,
                wide,
                total,
                total,
            ],
        ),
        out_shape=[
            jax.ShapeDtypeStruct(query_value.shape, BF16),
            jax.ShapeDtypeStruct(keys.shape, BF16),
        ],
        compiler_params=pltpu.CompilerParams(vmem_limit_bytes=40 << 20),
        name="attend_backward",
    )(first, kind, flip, segs[None, :], query_value, keys, attended, grad, lse)


def gelu_parts(values):
    below = 0.5 * (1.0 + lax.erf(values * (0.5 ** 0.5)))
    density = jnp.exp(values * values * -0.5) * ((2.0 * math.pi) ** -0.5)
    return values * below, below + values * density


def feed_forward_kernel(norm_ref, cot_ref, up_ref, down_ref, *refs):
    *earlier, mlp_ref, back_ref, up_grad_ref, down_grad_ref, act_ref, pre_ref = refs[:-1]
    sum_ref = mlp_ref if mlp_ref.dtype == F32 else refs[-1]
    rows = norm_ref.shape[0]
    chunk = min(rows, 256)

    @pl.when(pl.program_id(0) == 0)
    def _():
        sum_ref[...] = jnp.zeros(sum_ref.shape, F32)
        back_ref[...] = jnp.zeros(back_ref.shape, F32)

    for start in range(0, rows, chunk):
        at = slice(start, start + chunk)
        pre_act = dot(norm_ref[at, :], up_ref[...], NT)
        act_grad = dot(cot_ref[at, :], down_ref[...], NT)
        activation, slope = gelu_parts(pre_act)
        activation = activation.astype(BF16)
        pre_grad = (act_grad * slope).astype(BF16)
        act_ref[at, :] = activation
        pre_ref[at, :] = pre_grad
        sum_ref[at, :] += dot(activation, down_ref[...], NN)
        back_ref[at, :] += dot(pre_grad, up_ref[...], NN)
    up_grad = dot(pre_ref[...], norm_ref[...], TN)
    down_grad = dot(act_ref[...], cot_ref[...], TN)
    if earlier:
        up_grad = up_grad + earlier[0][...].astype(F32)
        down_grad = down_grad + earlier[1][...].astype(F32)
    up_grad_ref[...] = up_grad.astype(BF16)
    down_grad_ref[...] = down_grad.astype(BF16)

    if mlp_ref.dtype != F32:

        @pl.when(pl.program_id(0) == pl.num_programs(0) - 1)
        def _():
            mlp_ref[...] = sum_ref[...].astype(mlp_ref.dtype)


def feed_forward(norm, cot, up, down, earlier=(), kind=F32):
    rows, width = norm.shape
    hidden = up.shape[0]
    part = 512 if hidden % 512 == 0 else hidden
    whole = pl.BlockSpec((rows, width), lambda i: (0, 0))
    block = pl.BlockSpec((part, width), lambda i: (i, 0))
    grads = jax.ShapeDtypeStruct((hidden, width), BF16)
    return pl.pallas_call(
        feed_forward_kernel,
        grid=(hidden // part,),
        in_specs=[whole, whole, block, block] + [block] * len(earlier),
        out_specs=[whole, whole, block, block],
        out_shape=[
            jax.ShapeDtypeStruct((rows, width), kind),
            jax.ShapeDtypeStruct((rows, width), F32),
            grads,
            grads,
        ],
        scratch_shapes=[
            pltpu.VMEM((rows, part), BF16),
            pltpu.VMEM((rows, part), BF16),
            pltpu.VMEM((8, 128) if kind == F32 else (rows, width), F32),
        ],
        compiler_params=pltpu.CompilerParams(vmem_limit_bytes=58 << 20),
        name="feed_forward",
    )(norm, cot, up, down, *earlier)


def middle_kernel(parts, residual_ref, cot_ref, gain_ref, *refs):
    mlp_refs, back_refs = refs[:parts], refs[parts : 2 * parts]
    output_ref, res_grad_ref, branch_ref, norm_grad_ref = refs[2 * parts :]

    @pl.when(pl.program_id(0) == 0)
    def _():
        norm_grad_ref[...] = jnp.zeros(norm_grad_ref.shape, F32)

    residual = residual_ref[...]
    output_ref[...] = sum([ref[...].astype(F32) for ref in mlp_refs], residual).astype(BF16)
    grad = functools.reduce(jnp.add, [ref[...] for ref in back_refs])
    back, gain_grad, bias_grad = layer_norm_back(residual, gain_ref[...], grad)
    res_grad = cot_ref[...].astype(F32) + back
    res_grad_ref[...] = res_grad
    branch_ref[...] = res_grad.astype(BF16)
    norm_grad_ref[0:1, :] += gain_grad
    norm_grad_ref[1:2, :] += bias_grad


def middle(residual, cot, gain, mlps, backs):
    rows, width = residual.shape
    parts = len(mlps)
    step = 256
    block = pl.BlockSpec((step, width), lambda i: (i, 0))
    sums = jax.ShapeDtypeStruct((rows, width), F32)
    low = jax.ShapeDtypeStruct((rows, width), BF16)
    return pl.pallas_call(
        functools.partial(middle_kernel, parts),
        grid=(rows // step,),
        in_specs=[block, block, pl.BlockSpec((1, width), lambda i: (0, 0))] + [block] * (2 * parts),
        out_specs=[block, block, block, pl.BlockSpec((8, width), lambda i: (0, 0))],
        out_shape=[low, sums, low, jax.ShapeDtypeStruct((8, width), F32)],
        compiler_params=pltpu.CompilerParams(vmem_limit_bytes=40 << 20),
        name="middle",
    )(residual, cot, gain[None, :], *mlps, *backs)


def last_kernel(rows_ref, grad_ref, res_grad_ref, gain_ref, in_grad_ref, norm_grad_ref):
    @pl.when(pl.program_id(0) == 0)
    def _():
        norm_grad_ref[...] = jnp.zeros(norm_grad_ref.shape, F32)

    back, gain_grad, bias_grad = layer_norm_back(
        rows_ref[...].astype(F32), gain_ref[...], grad_ref[...]
    )
    in_grad_ref[...] = (res_grad_ref[...] + back).astype(BF16)
    norm_grad_ref[0:1, :] += gain_grad
    norm_grad_ref[1:2, :] += bias_grad


def last(rows_in, grad, res_grad, gain):
    rows, width = rows_in.shape
    step = 256
    block = pl.BlockSpec((step, width), lambda i: (i, 0))
    few = pl.BlockSpec((8, width), lambda i: (0, 0))
    return pl.pallas_call(
        last_kernel,
        grid=(rows // step,),
        in_specs=[block, block, block, pl.BlockSpec((1, width), lambda i: (0, 0))],
        out_specs=[block, few],
        out_shape=[
            jax.ShapeDtypeStruct((rows, width), BF16),
            jax.ShapeDtypeStruct((8, width), F32),
        ],
        compiler_params=pltpu.CompilerParams(vmem_limit_bytes=40 << 20),
        name="last",
    )(rows_in, grad, res_grad, gain[None, :])


def add(*terms):
    return functools.reduce(jnp.add, [item.astype(F32) for item in terms]).astype(BF16)


def swap(values, axis):
    name, size, mask = {
        "core": ("dp", 4, 1),
        "y": ("dp", 4, 2),
        "x": ("mp", 8, 1),
        "z1": ("mp", 8, 2),
        "z2": ("mp", 8, 4),
        "z3": ("mp", 8, 6),
    }[axis]
    return lax.ppermute(values, name, [(i, i ^ mask) for i in range(size)])


def order(at, mine, other):
    return jnp.where(at == 0, jnp.stack([mine, other]), jnp.stack([other, mine]))


class Line:
    def __init__(self):
        self.last = ()

    def __call__(self, step, *args):
        args, _ = lax.optimization_barrier((args, self.last))
        result = step(*args)
        self.last = tuple(jax.tree.leaves(result))
        return result


def on_cube(
    inputs,
    segments,
    ln1_gain,
    ln1_bias,
    w_query,
    w_key,
    w_value,
    w_output,
    ln2_gain,
    ln2_bias,
    w_up,
    w_down,
    cotangent,
):
    rows, width = inputs.shape
    local = w_query.shape[1]
    at_dp, at_mp = lax.axis_index("dp"), lax.axis_index("mp")
    at_y, at_core = at_dp // 2, at_dp % 2
    line = Line()

    def pick(values, at):
        return lax.dynamic_index_in_dim(values, at, 0, keepdims=False)

    def cut_attention(query, key, value, out):
        kinds = jnp.stack([query.T, key.T, value.T, out]).reshape(2, 2, 2, HEAD_DIM, width)
        return pick(kinds.transpose(0, 2, 1, 3, 4).reshape(4, 2, HEAD_DIM, width), at_dp)

    def cut_mlp(up, down):
        pieces = jnp.stack([up.T, down]).reshape(2, 4, -1, width)
        return lax.dynamic_index_in_dim(pieces, at_dp, 1, keepdims=False)

    def join(*parts):
        return jnp.concatenate(parts, 0)

    along_z = ("z2", "z1", "z3")
    attn_piece = line(cut_attention, w_query, w_key, w_value, w_output)
    attn_z = [swap(attn_piece, axis) for axis in along_z]
    mlp_piece = line(cut_mlp, w_up, w_down)
    mlp_z = [swap(mlp_piece, axis) for axis in along_z]

    def begin(rows_in):
        return layer_norm(rows_in.astype(F32), ln1_gain, ln1_bias).astype(BF16)

    norm_one = line(begin, inputs)
    segs = pick(segments, at_mp)
    place = windows(segs) + (at_y.reshape(1), segs)
    place = line(lambda item: item, place)

    near_z = line(lambda *parts: jnp.stack(parts[:4]), attn_piece, *attn_z, mlp_z[1])
    near_got = swap(near_z, "y")
    far_z = swap(near_z, "x")
    near_y = line(lambda *parts: jnp.stack(parts[:2]), near_z, near_got, far_z, mlp_z[0])
    near_got = swap(near_y, "core")
    far_got = swap(far_z, "y")

    def both_cores(mine, other):
        query_value, key_out = [jnp.stack([mine[:, :, i], other[:, :, i]]) for i in (0, 1)]
        key, out = [
            lax.dynamic_index_in_dim(key_out, at, 1, keepdims=False).reshape(-1, width)
            for at in (at_y, 1 - at_y)
        ]
        return query_value.reshape(-1, width), key, out

    def project(weights, norm):
        query_value = dot(weights[0], norm, NT).astype(BF16).reshape(2, 2, -1, rows)
        return query_value, dot(weights[1], norm, NT).astype(BF16).reshape(2, -1, rows)

    def attend(query_value, keys):
        return attend_forward(query_value, keys, place)

    def branch(base, attended, weights):
        return base + dot(attended.reshape(-1, rows), weights[2], TN)

    def mlp_along_z(*parts):
        return [jnp.concatenate([item[i] for item in parts], 0) for i in (0, 1)]

    def mlp_second(up, up_got, down, down_got):
        return jnp.concatenate([up, up_got], 0), jnp.stack([down, down_got])

    near_w = line(both_cores, near_y, near_got)
    near = line(project, near_w, norm_one)
    up, down = line(mlp_along_z, mlp_piece, *mlp_z)
    up_got, down_got = swap(up, "x"), swap(down, "y")
    near += tuple(line(attend, *near))

    far_y = line(lambda *parts: jnp.stack(parts), far_z, far_got)
    far_got = swap(far_y, "core")
    up, down = line(mlp_second, up, up_got, down, down_got)
    up_got, down_got = swap(up, "y"), swap(down, "x")
    residual = line(branch, inputs.astype(F32), near[2], near_w)
    far_w = line(both_cores, far_y, far_got)
    far = line(project, far_w, norm_one)
    far += tuple(line(attend, *far))

    def second_norm(residual, attended, weights):
        residual = branch(residual, attended, weights)
        return residual, layer_norm(residual, ln2_gain, ln2_bias).astype(BF16)

    cot_other = swap(cotangent, "core")
    far_attended, cot_other = lax.optimization_barrier((far[2], cot_other))
    residual, norm_two = line(second_norm, residual, far_attended, far_w)
    norm_two_other = swap(norm_two, "core")

    def mlp_last(up, up_got, down, down_got):
        return jnp.concatenate([up, up_got], 0), jnp.concatenate([down, down_got], 1).reshape(-1, width)

    up, down = line(mlp_last, up, up_got, down, down_got)
    mlp_b, back_b, *grads = line(
        lambda *args: feed_forward(*args, kind=BF16), norm_two_other, cot_other, up, down
    )
    mlp_b, back_b = swap(mlp_b, "core"), swap(back_b, "core")
    mlp_a, back_a, up_grad, down_grad = line(feed_forward, norm_two, cotangent, up, down, grads)

    def before_attention(attended, weights, grad):
        att_grad = dot(weights[2], grad, NT).astype(BF16).reshape(attended.shape)
        return att_grad, dot(attended.reshape(-1, rows), grad, NN).astype(BF16)


    quarter = up.shape[0] // 4

    def up_sum_of(terms, low, high):
        return add(*[item[low:high] for item in terms])

    def down_sum_of(terms, y, x, low=0, high=quarter):
        whole = terms[0].reshape(2, 2, quarter, width)[y, x, low:high]
        return add(whole, *[item.reshape(-1, quarter, width)[y, low:high] for item in terms[1:]])

    def mlp_sum_first(up_terms, down_terms):
        return (
            up_sum_of(up_terms, 2 * quarter, 4 * quarter),
            jnp.stack([down_sum_of(down_terms, y, 1) for y in (0, 1)]),
        )

    up_terms, down_terms = (up_grad,), (down_grad,)
    sends = line(mlp_sum_first, up_terms, down_terms)
    up_terms += (swap(sends[0], "y"),)
    down_terms += (swap(sends[1], "x"),)

    def attend_back(saved, att_grad):
        return attend_backward(*saved[:3], att_grad, saved[3], place)

    def weight_grads(query_value_grad, key_grad, out_grad, norm):
        query_value = dot(query_value_grad.reshape(-1, rows), norm, NN).astype(BF16)
        keys = dot(key_grad.reshape(-1, rows), norm, NN).astype(BF16)
        sums = (
            query_value.reshape(2, 2, -1, width),
            keys.reshape(2, -1, width),
            out_grad.reshape(2, -1, width),
        )
        return sums, [item[1] for item in sums]

    def project_back(grads, weights):
        return dot(grads[0].reshape(-1, rows), weights[0], TN) + dot(
            grads[1].reshape(-1, rows), weights[1], TN
        )

    def attn_terms_of(mine, got, at):
        terms = [(mine[0][0, at], mine[1][0], mine[2][0]), (got[0][at], got[1], got[2])]
        first = at_y == at
        return [
            [item[0] for item in terms],
            [jnp.where(first, item[1], item[2]) for item in terms],
        ]

    def sum_other_y(mine, got):
        return jnp.stack([add(*terms) for terms in attn_terms_of(mine, got, 1)])

    def sum_this_y(mine, got, from_y):
        terms = attn_terms_of(mine, got, 0)
        return jnp.stack([add(*terms[i], from_y[i]) for i in (0, 1)])

    output, res_grad, branch_grad, norm_two_grads = line(
        middle, residual, cotangent, ln2_gain, [mlp_a, mlp_b], [back_a, back_b]
    )
    far_att, far_out = line(before_attention, far[2], far_w, branch_grad)
    far_grads = line(attend_back, far, far_att)
    far_mine, sends = line(weight_grads, *far_grads, far_out, norm_one)
    far_got = [swap(item, "core") for item in sends]
    def mlp_sum_second(up_terms, down_terms):
        return up_sum_of(up_terms, quarter, 2 * quarter), down_sum_of(down_terms, 1, 0)

    sends = line(mlp_sum_second, up_terms, down_terms)
    up_terms += (swap(sends[0], "x"),)
    down_y = swap(sends[1], "y")

    norm_one_grad = line(project_back, far_grads, far_w)
    near_att, near_out = line(before_attention, near[2], near_w, branch_grad)
    far_y = swap(line(sum_other_y, far_mine, far_got), "y")

    part = quarter // 4

    def mlp_sum_of_z(up_terms, down_terms, down_y, low, high):
        low, high = low * part, high * part
        return jnp.stack(
            [
                up_sum_of(up_terms, low, high),
                down_sum_of(down_terms + (jnp.stack([down_y, down_y]),), 0, 0, low, high),
            ]
        )

    mlp_terms = (up_terms, down_terms, down_y)
    mlp_z1 = swap(line(lambda *terms: mlp_sum_of_z(*terms, 2, 4), *mlp_terms), "z1")
    near_grads = line(attend_back, near, near_att)
    mlp_send = line(
        lambda got, *terms: add(mlp_sum_of_z(*terms, 1, 2), got[:, part:]), mlp_z1, *mlp_terms
    )
    mlp_z2 = swap(mlp_send, "z2")
    near_mine, sends = line(weight_grads, *near_grads, near_out, norm_one)
    near_got = [swap(item, "core") for item in sends]
    far_x = swap(line(sum_this_y, far_mine, far_got, far_y), "x")
    near_y = swap(line(sum_other_y, near_mine, near_got), "y")

    def add_project_back(norm_one_grad, grads, weights):
        return norm_one_grad + project_back(grads, weights)

    def finish(norm_one_grad):
        in_grad, norm_one_grads = last(inputs, norm_one_grad, res_grad, ln1_gain)
        return jnp.concatenate([norm_one_grads[:2], norm_two_grads[:2]]), in_grad

    norm_one_grad = line(add_project_back, norm_one_grad, near_grads, near_w)
    norm_sums, in_grad = line(finish, norm_one_grad)
    got = swap(norm_sums, "core")

    mlp_sum = line(
        lambda got, other, *terms: add(mlp_sum_of_z(*terms, 0, 1), got[:, :part], other),
        mlp_z1,
        mlp_z2,
        *mlp_terms,
    )
    mlp_got = swap(mlp_sum, "y")
    norm_sums = line(jnp.add, norm_sums, got)
    got = swap(norm_sums, "y")

    def attn_sum_z(mine, got, from_y, from_x):
        from_x = from_x.reshape(2, -1, width)
        whole = sum_this_y(mine, got, from_y).astype(F32) + from_x
        return [whole[:, at * HEAD_DIM : (at + 1) * HEAD_DIM].astype(BF16) for at in range(4)]

    attn_mine, *sends = line(attn_sum_z, near_mine, near_got, near_y, far_x)
    attn_z = [swap(item, axis) for item, axis in zip(sends, along_z)]

    def in_order(piece, y, core, both):
        return order(at_core, order(at_y, piece, y), order(at_y, core, both))

    norm_sums = line(jnp.add, norm_sums, got)
    got = swap(norm_sums, "x")
    attn_sum = line(lambda _, *terms: add(*terms), mlp_got, attn_mine, *attn_z)
    attn_got = [
        lax.ppermute(attn_sum, "dp", [(i, i ^ mask) for i in range(4)]) for mask in (2, 1, 3)
    ]
    norm_sums = line(jnp.add, norm_sums, got)
    got = swap(norm_sums, "z1")
    mlp_sum = line(functools.partial(order, at_y), mlp_sum, mlp_got)
    mlp_got = swap(mlp_sum, "core")
    norm_sums = line(jnp.add, norm_sums, got)
    got = swap(norm_sums, "z2")
    attn_sum = line(in_order, attn_sum, *attn_got)
    attn_sum = line(
        lambda item: item.transpose(1, 2, 0, 3, 4).reshape(4, local, width).astype(F32), attn_sum
    )
    attn_sums = line(lambda item: (item[0].T, item[1].T, item[2].T, item[3]), attn_sum)
    norm_sums = line(jnp.add, norm_sums, got)
    mlp_sum = line(functools.partial(order, at_core), mlp_sum, mlp_got)
    up_sum, down_sum = line(
        lambda item: tuple(item.transpose(2, 1, 0, 3, 4).reshape(2, -1, width).astype(F32)), mlp_sum
    )
    up_sum = line(jnp.transpose, up_sum)
    norm_sums = lax.dynamic_slice_in_dim(norm_sums, at_mp * (width // 8), width // 8, 1)
    return (
        output,
        in_grad,
        norm_sums[0],
        norm_sums[1],
        *attn_sums,
        norm_sums[2],
        norm_sums[3],
        up_sum,
        down_sum,
    )


def on_any(
    mp_size,
    inputs,
    segments,
    ln1_gain,
    ln1_bias,
    w_query,
    w_key,
    w_value,
    w_output,
    ln2_gain,
    ln2_bias,
    w_up,
    w_down,
    cotangent,
):
    rows, width = inputs.shape
    seq_length = segments.shape[1]
    shared_by = seq_length // rows
    at_mp = lax.axis_index("mp")
    groups = [[start + i for i in range(shared_by)] for start in range(0, mp_size, shared_by)]

    def exchange(values, split, join):
        if shared_by == 1:
            return values
        return lax.all_to_all(values, "mp", split, join, axis_index_groups=groups, tiled=True)

    def gather(parts):
        return lax.all_gather(parts, "mp", axis=1, tiled=True)

    def reduce(parts):
        return lax.psum(lax.psum_scatter(parts, "mp", scatter_dimension=1, tiled=True), "dp")

    attn_w = gather(jnp.stack([w_query.T, w_value.T, w_key.T, w_output]))
    up, down = gather(jnp.stack([w_up.T, w_down]))
    project, w_out = attn_w[:3].reshape(3 * width, width), attn_w[3]

    segs = lax.dynamic_index_in_dim(segments, at_mp // shared_by, 0, keepdims=False)
    place = windows(segs) + (jnp.zeros((1,), jnp.int32), segs)
    resid_in = inputs.astype(F32)
    norm_one = layer_norm(resid_in, ln1_gain, ln1_bias).astype(BF16)
    projected = dot(project, norm_one, NT).astype(BF16).reshape(3, width, rows)
    projected = exchange(projected, 1, 2)
    query_value, keys = projected[None, :2], projected[2:]
    heads_out, lse = attend_forward(query_value, keys, place)
    attended = exchange(heads_out[0], 1, 0)
    residual = resid_in + dot(attended, w_out, TN)
    norm_two = layer_norm(residual, ln2_gain, ln2_bias).astype(BF16)
    mlp_branch, norm_two_grad, *mlp_grads = feed_forward(norm_two, cotangent, up, down)
    up_sum, down_sum = reduce(jnp.stack(mlp_grads)).astype(F32)

    output, res_grad, branch_grad, norm_two_grads = middle(
        residual, cotangent, ln2_gain, [mlp_branch], [norm_two_grad]
    )
    out_grad = dot(attended, branch_grad, NN).astype(BF16)
    att_grad = exchange(dot(w_out, branch_grad, NT).astype(BF16), 0, 1)
    query_value_grad, key_grad = attend_backward(
        query_value, keys, heads_out, att_grad[None], lse, place
    )
    proj_grad = exchange(jnp.concatenate([query_value_grad[0], key_grad]), 2, 1)
    proj_grad = proj_grad.reshape(3 * width, rows)
    project_grad = dot(proj_grad, norm_one, NN).astype(BF16).reshape(3, width, width)
    attn_sum = reduce(jnp.concatenate([project_grad, out_grad[None]])).astype(F32)
    in_grad, norm_one_grads = last(inputs, dot(proj_grad, project, TN), res_grad, ln1_gain)
    norm_parts = jnp.concatenate([norm_one_grads[:2], norm_two_grads[:2]])
    norm_sums = lax.dynamic_slice_in_dim(
        lax.psum(norm_parts, ("dp", "mp")), at_mp * (width // mp_size), width // mp_size, 1
    )
    return (
        output,
        in_grad,
        norm_sums[0],
        norm_sums[1],
        attn_sum[0].T,
        attn_sum[2].T,
        attn_sum[1].T,
        attn_sum[3],
        norm_sums[2],
        norm_sums[3],
        up_sum.T,
        down_sum,
    )


def shards(dp_size, mp_size, inputs, segments, *rest):
    if dp_size == 4 and mp_size == 8 and inputs.shape[0] == segments.shape[1]:
        return on_cube(inputs, segments, *rest)
    return on_any(mp_size, inputs, segments, *rest)


def solution(mesh):
    return jax.shard_map(
        functools.partial(shards, mesh.shape["dp"], mesh.shape["mp"]),
        mesh=mesh,
        in_specs=(
            P(("dp", "mp"), None),
            P("dp", None),
            P(),
            P(),
            P(None, "mp"),
            P(None, "mp"),
            P(None, "mp"),
            P("mp", None),
            P(),
            P(),
            P(None, "mp"),
            P("mp", None),
            P(("dp", "mp"), None),
        ),
        out_specs=(
            P(("dp", "mp"), None),
            P(("dp", "mp"), None),
            P("mp"),
            P("mp"),
            P(None, "mp"),
            P(None, "mp"),
            P(None, "mp"),
            P("mp", None),
            P("mp"),
            P("mp"),
            P(None, "mp"),
            P("mp", None),
        ),
        check_vma=False,
    )
```

profile of v0, /device:TPU:0, one launch (start us, length us, event | category | flops | bytes accessed | tf_op | source)
XLA Modules:
  0.0 276.7 jit_solution(8693416009470284105)
XLA Ops:
  2.0 4.1 %collective-permute-start = (bf16[2,48,768]{2,1,0:T(8,128)(2,1)S(1)}, bf16[2,48,768]{2,1,0:T(8,128)(2,1)}, u32[]{:S(2)}, u32[]{:S(2)}) collective-permute-start(bf16[2,48,768]{2,1,0:T(8,128)(2,1)S(1)} %dynamic-slice_bitcast_fusion), channel_id=1, source_target_pairs={{0,4},{1,5},{2,6},{3,7},{4,0},{5,1},{6,2},{7,3},{8,12},{9,13},{10,... | collective-permute-start | bytes 442376 | tf_op jit(solution)/shard_map/ppermute | solution.py:463
  6.1 1.6 collective-permute-start.1
  11.3 1.8 fusion.5
  13.3 1.6 collective-permute-done
  15.8 2.8 %collective-permute-done.2 = bf16[2,48,768]{2,1,0:T(8,128)(2,1)} collective-permute-done((bf16[2,48,768]{2,1,0:T(8,128)(2,1)S(1)}, bf16[2,48,768]{2,1,0:T(8,128)(2,1)}, u32[]{:S(2)}, u32[]{:S(2)}) %collective-permute-start.2) | collective-permute-done | bytes 147488 | tf_op jit(solution)/shard_map/ppermute | solution.py:463
  18.6 4.3 %collective-permute-done.3 = bf16[2,96,768]{2,1,0:T(8,128)(2,1)S(1)} collective-permute-done((bf16[2,96,768]{2,1,0:T(8,128)(2,1)S(1)}, bf16[2,96,768]{2,1,0:T(8,128)(2,1)S(1)}, u32[]{:S(2)}, u32[]{:S(2)}) %collective-permute-start.3) | collective-permute-done | bytes 294944 | tf_op jit(solution)/shard_map/ppermute | solution.py:463
  24.0 1.6 collective-permute-start.4
  25.7 1.5 collective-permute-start.5
  28.5 13.4 %collective-permute-done.6 = bf16[2,96,768]{2,1,0:T(8,128)(2,1)S(1)} collective-permute-done((bf16[2,96,768]{2,1,0:T(8,128)(2,1)S(1)}, bf16[2,96,768]{2,1,0:T(8,128)(2,1)S(1)}, u32[]{:S(2)}, u32[]{:S(2)}) %collective-permute-start.6) | collective-permute-done | bytes 294944 | tf_op jit(solution)/shard_map/ppermute | solution.py:463
  43.0 2.8 %collective-permute-start.8 = (bf16[2,96,768]{2,1,0:T(8,128)(2,1)S(1)}, bf16[2,96,768]{2,1,0:T(8,128)(2,1)}, u32[]{:S(2)}, u32[]{:S(2)}) collective-permute-start(bf16[2,96,768]{2,1,0:T(8,128)(2,1)S(1)} %fusion.29), channel_id=1, source_target_pairs={{0,6},{1,7},{2,4},{3,5},{4,2},{5,3},{6,0},{7,1},{8,14},{9,15},{10,... | collective-permute-start | bytes 884744 | tf_op jit(solution)/shard_map/ppermute | solution.py:463
  48.0 2.1 copy-done.34
  50.1 1.4 convolution_convert_fusion.1
  52.4 2.1 collective-permute-done.8
  56.8 8.9 %attend_forward.2 = (bf16[2,192,1024]{2,1,0:T(8,128)(2,1)S(1)}, f32[4,8,256]{2,1,0:T(8,128)S(1)}) custom-call(s32[8]{0:T(128)S(1)} %subtract_minimum_fusion.first_ref, s32[8]{0:T(128)S(1)} %select_reduce_fusion.kind_ref, s32[1]{0:T(128)} %bitcast.2.flip_ref, s32[1,1024]{1,0:T(1,128)S(1)} %constant_dynamic-slice_fusion.1, ...), custom_call_target="tpu_custom_call" | custom-call | tf_op jit(solution)/shard_map/attend_forward/pallas_call | solution.py:256
  66.0 1.5 copy-done.4
  67.7 6.4 %collective-permute-done.10 = bf16[384,768]{1,0:T(8,128)(2,1)S(1)} collective-permute-done((bf16[384,768]{1,0:T(8,128)(2,1)S(1)}, bf16[384,768]{1,0:T(8,128)(2,1)S(1)}, u32[]{:S(2)}, u32[]{:S(2)}) %collective-permute-start.10) | collective-permute-done | bytes 589856 | tf_op jit(solution)/shard_map/ppermute | solution.py:463
  78.4 1.4 convolution_convert_fusion
  79.8 8.6 %attend_forward.3 = (bf16[2,192,1024]{2,1,0:T(8,128)(2,1)S(1)}, f32[4,8,256]{2,1,0:T(8,128)S(1)}) custom-call(s32[8]{0:T(128)S(1)} %subtract_minimum_fusion.first_ref, s32[8]{0:T(128)S(1)} %select_reduce_fusion.kind_ref, s32[1]{0:T(128)} %bitcast.2.flip_ref, s32[1,1024]{1,0:T(1,128)S(1)} %constant_dynamic-slice_fusion.1, ...), custom_call_target="tpu_custom_call" | custom-call | tf_op jit(solution)/shard_map/attend_forward/pallas_call | solution.py:256
  91.3 10.2 %collective-permute-done.15 = bf16[2,384,768]{2,1,0:T(8,128)(2,1)S(1)} collective-permute-done((bf16[2,384,768]{2,1,0:T(8,128)(2,1)S(1)}, bf16[2,384,768]{2,1,0:T(8,128)(2,1)S(1)}, u32[]{:S(2)}, u32[]{:S(2)}) %collective-permute-start.15) | collective-permute-done | bytes 1179680 | tf_op jit(solution)/shard_map/ppermute | solution.py:463
  102.5 1.4 constant_dynamic-update-slice_fusion.2.up_ref
  104.2 1.7 pad_maximum_fusion
  107.5 21.8 %feed_forward.2 = (bf16[1024,768]{1,0:T(8,128)(2,1)}, f32[1024,768]{1,0:T(8,128)}, bf16[1536,768]{1,0:T(8,128)(2,1)}, bf16[1536,768]{1,0:T(8,128)(2,1)}) custom-call(bf16[1024,768]{1,0:T(8,128)(2,1)} %copy-done.38, bf16[1024,768]{1,0:T(8,128)(2,1)} %copy-done.37, bf16[1536,768]{1,0:T(8,128)(2,1)} %copy-done.22, bf16[1536,768]{1,0:T(8,128)(2,1)} %bitcast.278), custom_call_target="tpu_custom_call" | custom-call | tf_op jit(solution)/shard_map/feed_forward/pallas_call | solution.py:360
  129.8 20.8 %feed_forward.3 = (f32[1024,768]{1,0:T(8,128)}, f32[1024,768]{1,0:T(8,128)}, bf16[1536,768]{1,0:T(8,128)(2,1)}, bf16[1536,768]{1,0:T(8,128)(2,1)}) custom-call(bf16[1024,768]{1,0:T(8,128)(2,1)} %copy-done.24, bf16[1024,768]{1,0:T(8,128)(2,1)} %cot_ref.1, bf16[1536,768]{1,0:T(8,128)(2,1)} %copy-done.22, bf16[1536,768]{1,0:T(8,128)(2,1)} %bitcast.279, ...), custom_call_target="tpu_custom_call" | custom-call | tf_op jit(solution)/shard_map/feed_forward/pallas_call | solution.py:360
  150.6 1.5 slice.285
  155.1 5.9 %middle.1 = (bf16[1024,768]{1,0:T(8,128)(2,1)}, f32[1024,768]{1,0:T(8,128)S(1)}, bf16[1024,768]{1,0:T(8,128)(2,1)S(1)}, f32[8,768]{1,0:T(8,128)S(1)}) custom-call(f32[1024,768]{1,0:T(8,128)S(1)} %get-tuple-element.291.residual_ref, bf16[1024,768]{1,0:T(8,128)(2,1)S(1)} %copy-done.5, f32[1,768]{1,0:T(1,128)S(1)} %broadcast_in_dim.18.gain_ref, ...), custom_call_target="tpu_custom_call" | custom-call | tf_op jit(solution)/shard_map/middle/pallas_call | solution.py:407
  164.5 13.9 %attend_backward.2 = (bf16[2,2,192,1024]{3,2,1,0:T(8,128)(2,1)S(1)}, bf16[2,192,1024]{2,1,0:T(8,128)(2,1)S(1)}) custom-call(s32[8]{0:T(128)S(1)} %subtract_minimum_fusion.first_ref, s32[8]{0:T(128)S(1)} %select_reduce_fusion.kind_ref, s32[1]{0:T(128)} %bitcast.2.flip_ref, s32[1,1024]{1,0:T(1,128)S(1)} %constant_dynamic-slice_fusion.1, ...), custom_call_target="tpu_custom_call" | custom-call | tf_op jit(solution)/shard_map/attend_backward/pallas_call | solution.py:284
  182.3 1.5 add_convert_fusion.2
  184.9 1.4 fusion.40
  186.4 2.6 convolution_add_fusion
  189.0 1.6 convolution_convert_fusion.9
  190.6 1.7 convolution_convert_fusion.4
  193.5 3.8 %collective-permute-done.22 = bf16[384,768]{1,0:T(8,128)(2,1)S(1)} collective-permute-done((bf16[384,768]{1,0:T(8,128)(2,1)S(1)}, bf16[384,768]{1,0:T(8,128)(2,1)S(1)}, u32[]{:S(2)}, u32[]{:S(2)}) %collective-permute-start.22) | collective-permute-done | bytes 589856 | tf_op jit(solution)/shard_map/ppermute | solution.py:463
  197.3 2.2 collective-permute-done.21
  204.9 13.8 %attend_backward.3 = (bf16[2,2,192,1024]{3,2,1,0:T(8,128)(2,1)S(1)}, bf16[2,192,1024]{2,1,0:T(8,128)(2,1)S(1)}) custom-call(s32[8]{0:T(128)S(1)} %subtract_minimum_fusion.first_ref, s32[8]{0:T(128)S(1)} %select_reduce_fusion.kind_ref, s32[1]{0:T(128)} %bitcast.2.flip_ref, s32[1,1024]{1,0:T(1,128)S(1)} %constant_dynamic-slice_fusion.1, ...), custom_call_target="tpu_custom_call" | custom-call | tf_op jit(solution)/shard_map/attend_backward/pallas_call | solution.py:284
  222.9 1.4 convolution_convert_fusion.2
  227.7 1.9 collective-permute-start.34
  229.6 1.4 fusion.41
  234.0 3.4 %last.1 = (bf16[1024,768]{1,0:T(8,128)(2,1)}, f32[8,768]{1,0:T(8,128)S(1)}) custom-call(bf16[1024,768]{1,0:T(8,128)(2,1)S(1)} %copy-done.3, f32[1024,768]{1,0:T(8,128)S(1)} %add_add_fusion.grad_ref, f32[1024,768]{1,0:T(8,128)S(1)} %copy-done.11, f32[1,768]{1,0:T(1,128)S(1)} %broadcast_in_dim.19.gain_ref), custom_call_target="tpu_custom_call" | custom-call | tf_op jit(solution)/shard_map/last/pallas_call | solution.py:436
  243.6 3.0 %collective-permute-start.38 = (bf16[2,48,768]{2,1,0:T(8,128)(2,1)S(1)}, bf16[2,48,768]{2,1,0:T(8,128)(2,1)S(1)}, u32[]{:S(2)}, u32[]{:S(2)}) collective-permute-start(bf16[2,48,768]{2,1,0:T(8,128)(2,1)S(1)} %get-tuple-element.476), channel_id=1, source_target_pairs={{0,4},{1,5},{2,6},{3,7},{4,0},{5,1},{6,2},{7,3},{8,12},{9,13},{10,... | collective-permute-start | bytes 442376 | tf_op jit(solution)/shard_map/ppermute | solution.py:463
  247.1 1.7 collective-permute-start.40
  249.8 2.7 collective-permute-done.33
  252.5 3.7 %collective-permute-done.38 = bf16[2,48,768]{2,1,0:T(8,128)(2,1)S(1)} collective-permute-done((bf16[2,48,768]{2,1,0:T(8,128)(2,1)S(1)}, bf16[2,48,768]{2,1,0:T(8,128)(2,1)S(1)}, u32[]{:S(2)}, u32[]{:S(2)}) %collective-permute-start.38) | collective-permute-done | bytes 147488 | tf_op jit(solution)/shard_map/ppermute | solution.py:463
  256.1 1.6 collective-permute-done.40
  258.4 1.6 collective-permute-start.45
  260.7 3.0 %collective-permute-done.36 = f32[4,768]{1,0:T(4,128)S(1)} collective-permute-done((f32[4,768]{1,0:T(4,128)S(1)}, f32[4,768]{1,0:T(4,128)S(1)}, u32[]{:S(2)}, u32[]{:S(2)}) %collective-permute-start.36) | collective-permute-done | bytes 12320 | tf_op jit(solution)/shard_map/ppermute | solution.py:463
  263.7 2.2 collective-permute-start.41
  266.1 1.5 collective-permute-done.41
  267.6 3.2 %collective-permute-start.42 = (f32[4,768]{1,0:T(4,128)S(1)}, f32[4,768]{1,0:T(4,128)S(1)}, u32[]{:S(2)}, u32[]{:S(2)}) collective-permute-start(f32[4,768]{1,0:T(4,128)S(1)} %add.271), channel_id=1, source_target_pairs={{0,4},{1,5},{2,6},{3,7},{4,0},{5,1},{6,2},{7,3},{8,12},{9,13},{10,... | collective-permute-start | bytes 36872 | tf_op jit(solution)/shard_map/ppermute | solution.py:463
  (318 shorter events, 68.2 us)
Async XLA Ops:
  2.0 12.9 %collective-permute-start = (bf16[2,48,768]{2,1,0:T(8,128)(2,1)S(1)}, bf16[2,48,768]{2,1,0:T(8,128)(2,1)}, u32[]{:S(2)}, u32[]{:S(2)}) collective-permute-start(bf16[2,48,768]{2,1,0:T(8,128)(2,1)S(1)} %dynamic-slice_bitcast_fusion), channel_id=1, source_target_pairs={{0,4},{1,5},{2,6},{3,7},{4,0},{5,1},{6,2},{7,3},{8,12},{9,13},{10,... | collective-permute-start | bytes 442376 | tf_op jit(solution)/shard_map/ppermute | solution.py:463
  6.1 9.7 %collective-permute-start.1 = (bf16[2,48,768]{2,1,0:T(8,128)(2,1)S(1)}, bf16[2,48,768]{2,1,0:T(8,128)(2,1)}, u32[]{:S(2)}, u32[]{:S(2)}) collective-permute-start(bf16[2,48,768]{2,1,0:T(8,128)(2,1)S(1)} %dynamic-slice_bitcast_fusion), channel_id=1, source_target_pairs={{0,2},{1,3},{2,0},{3,1},{4,6},{5,7},{6,4},{7,5},{8,10},{9,11},{10,... | collective-permute-start | bytes 442376 | tf_op jit(solution)/shard_map/ppermute | solution.py:463
  7.7 10.9 %collective-permute-start.2 = (bf16[2,48,768]{2,1,0:T(8,128)(2,1)S(1)}, bf16[2,48,768]{2,1,0:T(8,128)(2,1)}, u32[]{:S(2)}, u32[]{:S(2)}) collective-permute-start(bf16[2,48,768]{2,1,0:T(8,128)(2,1)S(1)} %dynamic-slice_bitcast_fusion), channel_id=1, source_target_pairs={{0,6},{1,7},{2,4},{3,5},{4,2},{5,3},{6,0},{7,1},{8,14},{9,15},{10,... | collective-permute-start | bytes 442376 | tf_op jit(solution)/shard_map/ppermute | solution.py:463
  8.9 14.0 %collective-permute-start.3 = (bf16[2,96,768]{2,1,0:T(8,128)(2,1)S(1)}, bf16[2,96,768]{2,1,0:T(8,128)(2,1)S(1)}, u32[]{:S(2)}, u32[]{:S(2)}) collective-permute-start(bf16[2,96,768]{2,1,0:T(8,128)(2,1)S(1)} %fusion.29), channel_id=1, source_target_pairs={{0,2},{1,3},{2,0},{3,1},{4,6},{5,7},{6,4},{7,5},{8,10},{9,11},{10,... | collective-permute-start | bytes 884744 | tf_op jit(solution)/shard_map/ppermute | solution.py:463
  24.0 17.9 %collective-permute-start.4 = (bf16[4,2,48,768]{3,2,0,1:T(8,128)(2,1)S(1)}, bf16[4,2,48,768]{3,2,0,1:T(8,128)(2,1)S(1)}, u32[]{:S(2)}, u32[]{:S(2)}) collective-permute-start(bf16[4,2,48,768]{3,2,0,1:T(8,128)(2,1)S(1)} %pad_maximum_fusion.8), channel_id=1, source_target_pairs={{0,16},{8,24},{16,0},{24,8},{1,17},{9,25},{17,1},{25,9},{2,18},{10... | collective-permute-start | bytes 1769480 | tf_op jit(solution)/shard_map/ppermute | solution.py:463
  25.7 16.2 %collective-permute-start.5 = (bf16[4,2,48,768]{3,2,0,1:T(8,128)(2,1)S(1)}, bf16[4,2,48,768]{3,2,0,1:T(8,128)(2,1)S(1)}, u32[]{:S(2)}, u32[]{:S(2)}) collective-permute-start(bf16[4,2,48,768]{3,2,0,1:T(8,128)(2,1)S(1)} %pad_maximum_fusion.8), channel_id=1, source_target_pairs={{0,1},{1,0},{2,3},{3,2},{4,5},{5,4},{6,7},{7,6},{8,9},{9,8},{10,11... | collective-permute-start | bytes 1769480 | tf_op jit(solution)/shard_map/ppermute | solution.py:463
  27.2 14.7 %collective-permute-start.6 = (bf16[2,96,768]{2,1,0:T(8,128)(2,1)S(1)}, bf16[2,96,768]{2,1,0:T(8,128)(2,1)S(1)}, u32[]{:S(2)}, u32[]{:S(2)}) collective-permute-start(bf16[2,96,768]{2,1,0:T(8,128)(2,1)S(1)} %fusion.29), channel_id=1, source_target_pairs={{0,4},{1,5},{2,6},{3,7},{4,0},{5,1},{6,2},{7,3},{8,12},{9,13},{10,... | collective-permute-start | bytes 884744 | tf_op jit(solution)/shard_map/ppermute | solution.py:463
  42.9 3.4 %collective-permute-start.7 = (bf16[2,4,2,48,768]{4,3,1,0,2:T(8,128)(2,1)S(1)}, bf16[2,4,2,48,768]{4,3,1,0,2:T(8,128)(2,1)}, u32[]{:S(2)}, u32[]{:S(2)}) collective-permute-start(bf16[2,4,2,48,768]{4,3,1,0,2:T(8,128)(2,1)S(1)} %pad_maximum_fusion.1), channel_id=1, source_target_pairs={{0,8},{8,0},{16,24},{24,16},{1,9},{9,1},{17,25},{25,17},{2,10},{10... | collective-permute-start | bytes 3538952 | tf_op jit(solution)/shard_map/ppermute | solution.py:463
  43.0 11.4 %collective-permute-start.8 = (bf16[2,96,768]{2,1,0:T(8,128)(2,1)S(1)}, bf16[2,96,768]{2,1,0:T(8,128)(2,1)}, u32[]{:S(2)}, u32[]{:S(2)}) collective-permute-start(bf16[2,96,768]{2,1,0:T(8,128)(2,1)S(1)} %fusion.29), channel_id=1, source_target_pairs={{0,6},{1,7},{2,4},{3,5},{4,2},{5,3},{6,0},{7,1},{8,14},{9,15},{10,... | collective-permute-start | bytes 884744 | tf_op jit(solution)/shard_map/ppermute | solution.py:463
  45.8 19.9 %collective-permute-start.11 = (bf16[4,2,48,768]{3,2,0,1:T(8,128)(2,1)}, bf16[4,2,48,768]{3,2,0,1:T(8,128)(2,1)S(1)}, u32[]{:S(2)}, u32[]{:S(2)}) collective-permute-start(bf16[4,2,48,768]{3,2,0,1:T(8,128)(2,1)} %copy-done.62), channel_id=1, source_target_pairs={{0,16},{8,24},{16,0},{24,8},{1,17},{9,25},{17,1},{25,9},{2,18},{10... | collective-permute-start | bytes 1769480 | tf_op jit(solution)/shard_map/ppermute | solution.py:463
  55.6 18.4 %collective-permute-start.10 = (bf16[384,768]{1,0:T(8,128)(2,1)S(1)}, bf16[384,768]{1,0:T(8,128)(2,1)S(1)}, u32[]{:S(2)}, u32[]{:S(2)}) collective-permute-start(bf16[384,768]{1,0:T(8,128)(2,1)S(1)} %pad_maximum_fusion.10), channel_id=1, source_target_pairs={{0,16},{8,24},{16,0},{24,8},{1,17},{9,25},{17,1},{25,9},{2,18},{10... | collective-permute-start | bytes 1769480 | tf_op jit(solution)/shard_map/ppermute | solution.py:463
  56.2 17.8 %collective-permute-start.9 = (bf16[384,768]{1,0:T(8,128)(2,1)S(1)}, bf16[384,768]{1,0:T(8,128)(2,1)S(1)}, u32[]{:S(2)}, u32[]{:S(2)}) collective-permute-start(bf16[384,768]{1,0:T(8,128)(2,1)S(1)} %pad_maximum_fusion.9), channel_id=1, source_target_pairs={{0,1},{1,0},{2,3},{3,2},{4,5},{5,4},{6,7},{7,6},{8,9},{9,8},{10,11... | collective-permute-start | bytes 1769480 | tf_op jit(solution)/shard_map/ppermute | solution.py:463
  65.9 10.6 %collective-permute-start.12 = (bf16[2,4,2,48,768]{4,3,1,0,2:T(8,128)(2,1)S(1)}, bf16[2,4,2,48,768]{4,3,1,0,2:T(8,128)(2,1)S(1)}, u32[]{:S(2)}, u32[]{:S(2)}) collective-permute-start(bf16[2,4,2,48,768]{4,3,1,0,2:T(8,128)(2,1)S(1)} %pad_maximum_fusion.3), channel_id=1, source_target_pairs={{0,8},{8,0},{16,24},{24,16},{1,9},{9,1},{17,25},{25,17},{2,10},{10... | collective-permute-start | bytes 3538952 | tf_op jit(solution)/shard_map/ppermute | solution.py:463
  67.4 21.0 %collective-permute-start.13 = (bf16[1024,768]{1,0:T(8,128)(2,1)S(1)}, bf16[1024,768]{1,0:T(8,128)(2,1)S(1)}, u32[]{:S(2)}, u32[]{:S(2)}) collective-permute-start(bf16[1024,768]{1,0:T(8,128)(2,1)S(1)} %copy-done.4), channel_id=1, source_target_pairs={{0,8},{8,0},{16,24},{24,16},{1,9},{9,1},{17,25},{25,17},{2,10},{10... | collective-permute-start | bytes 4718600 | tf_op jit(solution)/shard_map/ppermute | solution.py:463
  74.2 27.3 %collective-permute-start.15 = (bf16[2,384,768]{2,1,0:T(8,128)(2,1)S(1)}, bf16[2,384,768]{2,1,0:T(8,128)(2,1)S(1)}, u32[]{:S(2)}, u32[]{:S(2)}) collective-permute-start(bf16[2,384,768]{2,1,0:T(8,128)(2,1)S(1)} %pad_maximum_fusion.4), channel_id=1, source_target_pairs={{0,1},{1,0},{2,3},{3,2},{4,5},{5,4},{6,7},{7,6},{8,9},{9,8},{10,11... | collective-permute-start | bytes 3538952 | tf_op jit(solution)/shard_map/ppermute | solution.py:463
  74.9 27.6 %collective-permute-start.14 = (bf16[768,768]{1,0:T(8,128)(2,1)S(1)}, bf16[768,768]{1,0:T(8,128)(2,1)}, u32[]{:S(2)}, u32[]{:S(2)}) collective-permute-start(bf16[768,768]{1,0:T(8,128)(2,1)S(1)} %constant_dynamic-update-slice_fusion), channel_id=1, source_target_pairs={{0,16},{8,24},{16,0},{24,8},{1,17},{9,25},{17,1},{25,9},{2,18},{10... | collective-permute-start | bytes 3538952 | tf_op jit(solution)/shard_map/ppermute | solution.py:463
  91.2 15.2 %collective-permute-start.16 = (bf16[1024,768]{1,0:T(8,128)(2,1)S(1)}, bf16[1024,768]{1,0:T(8,128)(2,1)S(1)}, u32[]{:S(2)}, u32[]{:S(2)}) collective-permute-start(bf16[1024,768]{1,0:T(8,128)(2,1)S(1)} %add_convert_fusion.norm_ref), channel_id=1, source_target_pairs={{0,8},{8,0},{16,24},{24,16},{1,9},{9,1},{17,25},{25,17},{2,10},{10... | collective-permute-start | bytes 4718600 | tf_op jit(solution)/shard_map/ppermute | solution.py:463
  129.3 25.1 %collective-permute-start.18 = (f32[1024,768]{1,0:T(8,128)}, f32[1024,768]{1,0:T(8,128)}, u32[]{:S(2)}, u32[]{:S(2)}) collective-permute-start(f32[1024,768]{1,0:T(8,128)} %get-tuple-element.278), channel_id=1, source_target_pairs={{0,8},{8,0},{16,24},{24,16},{1,9},{9,1},{17,25},{25,17},{2,10},{10... | collective-permute-start | bytes 9437192 | tf_op jit(solution)/shard_map/ppermute | solution.py:463
  129.3 25.1 %collective-permute-start.17 = (bf16[1024,768]{1,0:T(8,128)(2,1)}, bf16[1024,768]{1,0:T(8,128)(2,1)}, u32[]{:S(2)}, u32[]{:S(2)}) collective-permute-start(bf16[1024,768]{1,0:T(8,128)(2,1)} %get-tuple-element.277), channel_id=1, source_target_pairs={{0,8},{8,0},{16,24},{24,16},{1,9},{9,1},{17,25},{25,17},{2,10},{10... | collective-permute-start | bytes 4718600 | tf_op jit(solution)/shard_map/ppermute | solution.py:463
  152.9 28.5 %collective-permute-start.20 = (bf16[2,384,768]{2,1,0:T(8,128)(2,1)S(1)}, bf16[2,384,768]{2,1,0:T(8,128)(2,1)S(1)}, u32[]{:S(2)}, u32[]{:S(2)}) collective-permute-start(bf16[2,384,768]{2,1,0:T(8,128)(2,1)S(1)} %pad_maximum_fusion.6), channel_id=1, source_target_pairs={{0,1},{1,0},{2,3},{3,2},{4,5},{5,4},{6,7},{7,6},{8,9},{9,8},{10,11... | collective-permute-start | bytes 3538952 | tf_op jit(solution)/shard_map/ppermute | solution.py:463
  153.9 27.7 %collective-permute-start.19 = (bf16[768,768]{1,0:T(8,128)(2,1)S(1)}, bf16[768,768]{1,0:T(8,128)(2,1)S(1)}, u32[]{:S(2)}, u32[]{:S(2)}) collective-permute-start(bf16[768,768]{1,0:T(8,128)(2,1)S(1)} %slice.285), channel_id=1, source_target_pairs={{0,16},{8,24},{16,0},{24,8},{1,17},{9,25},{17,1},{25,9},{2,18},{10... | collective-permute-start | bytes 3538952 | tf_op jit(solution)/shard_map/ppermute | solution.py:463
  162.7 29.8 %copy-start.40 = (bf16[384,768]{1,0:T(8,128)(2,1)}, bf16[384,768]{1,0:T(8,128)(2,1)S(1)}, u32[]{:S(2)}) copy-start(bf16[384,768]{1,0:T(8,128)(2,1)S(1)} %convolution_convert_fusion.11) | copy-start | bytes 1769476
  180.7 11.6 %collective-permute-start.23 = (bf16[2,192,768]{2,1,0:T(8,128)(2,1)S(1)}, bf16[2,192,768]{2,1,0:T(8,128)(2,1)S(1)}, u32[]{:S(2)}, u32[]{:S(2)}) collective-permute-start(bf16[2,192,768]{2,1,0:T(8,128)(2,1)S(1)} %bitcast.322), channel_id=1, source_target_pairs={{0,8},{8,0},{16,24},{24,16},{1,9},{9,1},{17,25},{25,17},{2,10},{10... | collective-permute-start | bytes 1769480 | tf_op jit(solution)/shard_map/ppermute | solution.py:463
  180.8 11.5 %collective-permute-start.24 = (bf16[192,768]{1,0:T(8,128)(2,1)S(1)}, bf16[192,768]{1,0:T(8,128)(2,1)S(1)}, u32[]{:S(2)}, u32[]{:S(2)}) collective-permute-start(bf16[192,768]{1,0:T(8,128)(2,1)S(1)} %slice.357), channel_id=1, source_target_pairs={{0,8},{8,0},{16,24},{24,16},{1,9},{9,1},{17,25},{25,17},{2,10},{10... | collective-permute-start | bytes 884744 | tf_op jit(solution)/shard_map/ppermute | solution.py:463
  181.3 11.0 %collective-permute-start.25 = (bf16[192,768]{1,0:T(8,128)(2,1)S(1)}, bf16[192,768]{1,0:T(8,128)(2,1)S(1)}, u32[]{:S(2)}, u32[]{:S(2)}) collective-permute-start(bf16[192,768]{1,0:T(8,128)(2,1)S(1)} %slice.290), channel_id=1, source_target_pairs={{0,8},{8,0},{16,24},{24,16},{1,9},{9,1},{17,25},{25,17},{2,10},{10... | collective-permute-start | bytes 884744 | tf_op jit(solution)/shard_map/ppermute | solution.py:463
  181.7 15.5 %collective-permute-start.22 = (bf16[384,768]{1,0:T(8,128)(2,1)S(1)}, bf16[384,768]{1,0:T(8,128)(2,1)S(1)}, u32[]{:S(2)}, u32[]{:S(2)}) collective-permute-start(bf16[384,768]{1,0:T(8,128)(2,1)S(1)} %fusion.6), channel_id=1, source_target_pairs={{0,16},{8,24},{16,0},{24,8},{1,17},{9,25},{17,1},{25,9},{2,18},{10... | collective-permute-start | bytes 1769480 | tf_op jit(solution)/shard_map/ppermute | solution.py:463
  183.8 15.7 %collective-permute-start.21 = (bf16[384,768]{1,0:T(8,128)(2,1)S(1)}, bf16[384,768]{1,0:T(8,128)(2,1)S(1)}, u32[]{:S(2)}, u32[]{:S(2)}) collective-permute-start(bf16[384,768]{1,0:T(8,128)(2,1)S(1)} %add_convert_fusion.2), channel_id=1, source_target_pairs={{0,1},{1,0},{2,3},{3,2},{4,5},{5,4},{6,7},{7,6},{8,9},{9,8},{10,11... | collective-permute-start | bytes 1769480 | tf_op jit(solution)/shard_map/ppermute | solution.py:463
  201.9 16.9 %collective-permute-start.26 = (bf16[2,192,768]{2,1,0:T(8,128)(2,1)}, bf16[2,192,768]{2,1,0:T(8,128)(2,1)}, u32[]{:S(2)}, u32[]{:S(2)}) collective-permute-start(bf16[2,192,768]{2,1,0:T(8,128)(2,1)} %pad_maximum_fusion.12), channel_id=1, source_target_pairs={{0,2},{1,3},{2,0},{3,1},{4,6},{5,7},{6,4},{7,5},{8,10},{9,11},{10,... | collective-permute-start | bytes 1769480 | tf_op jit(solution)/shard_map/ppermute | solution.py:463
  202.5 22.6 %collective-permute-start.30 = (bf16[2,192,768]{2,1,0:T(8,128)(2,1)}, bf16[2,192,768]{2,1,0:T(8,128)(2,1)S(1)}, u32[]{:S(2)}, u32[]{:S(2)}) collective-permute-start(bf16[2,192,768]{2,1,0:T(8,128)(2,1)} %pad_maximum_fusion.11), channel_id=1, source_target_pairs={{0,16},{8,24},{16,0},{24,8},{1,17},{9,25},{17,1},{25,9},{2,18},{10... | collective-permute-start | bytes 1769480 | tf_op jit(solution)/shard_map/ppermute | solution.py:463
  222.0 15.5 %collective-permute-start.32 = (bf16[2,96,768]{2,1,0:T(8,128)(2,1)S(1)}, bf16[2,96,768]{2,1,0:T(8,128)(2,1)S(1)}, u32[]{:S(2)}, u32[]{:S(2)}) collective-permute-start(bf16[2,96,768]{2,1,0:T(8,128)(2,1)S(1)} %add_convert_fusion.4), channel_id=1, source_target_pairs={{0,4},{1,5},{2,6},{3,7},{4,0},{5,1},{6,2},{7,3},{8,12},{9,13},{10,... | collective-permute-start | bytes 884744 | tf_op jit(solution)/shard_map/ppermute | solution.py:463
  224.4 3.0 %collective-permute-start.27 = (bf16[2,192,768]{2,1,0:T(8,128)(2,1)S(1)}, bf16[2,192,768]{2,1,0:T(8,128)(2,1)S(1)}, u32[]{:S(2)}, u32[]{:S(2)}) collective-permute-start(bf16[2,192,768]{2,1,0:T(8,128)(2,1)S(1)} %bitcast.323), channel_id=1, source_target_pairs={{0,8},{8,0},{16,24},{24,16},{1,9},{9,1},{17,25},{25,17},{2,10},{10... | collective-permute-start | bytes 1769480 | tf_op jit(solution)/shard_map/ppermute | solution.py:463
  224.5 2.9 %collective-permute-start.28 = (bf16[192,768]{1,0:T(8,128)(2,1)S(1)}, bf16[192,768]{1,0:T(8,128)(2,1)S(1)}, u32[]{:S(2)}, u32[]{:S(2)}) collective-permute-start(bf16[192,768]{1,0:T(8,128)(2,1)S(1)} %slice.364), channel_id=1, source_target_pairs={{0,8},{8,0},{16,24},{24,16},{1,9},{9,1},{17,25},{25,17},{2,10},{10... | collective-permute-start | bytes 884744 | tf_op jit(solution)/shard_map/ppermute | solution.py:463
  225.0 2.4 collective-permute-start.29
  227.0 15.2 %collective-permute-start.35 = (bf16[2,192,768]{2,1,0:T(8,128)(2,1)S(1)}, bf16[2,192,768]{2,1,0:T(8,128)(2,1)S(1)}, u32[]{:S(2)}, u32[]{:S(2)}) collective-permute-start(bf16[2,192,768]{2,1,0:T(8,128)(2,1)S(1)} %pad_maximum_fusion.13), channel_id=1, source_target_pairs={{0,1},{1,0},{2,3},{3,2},{4,5},{5,4},{6,7},{7,6},{8,9},{9,8},{10,11... | collective-permute-start | bytes 1769480 | tf_op jit(solution)/shard_map/ppermute | solution.py:463
  227.7 15.4 %collective-permute-start.34 = (bf16[2,192,768]{2,1,0:T(8,128)(2,1)S(1)}, bf16[2,192,768]{2,1,0:T(8,128)(2,1)S(1)}, u32[]{:S(2)}, u32[]{:S(2)}) collective-permute-start(bf16[2,192,768]{2,1,0:T(8,128)(2,1)S(1)} %pad_maximum_fusion.14), channel_id=1, source_target_pairs={{0,16},{8,24},{16,0},{24,8},{1,17},{9,25},{17,1},{25,9},{2,18},{10... | collective-permute-start | bytes 1769480 | tf_op jit(solution)/shard_map/ppermute | solution.py:463
  237.4 3.5 %collective-permute-start.31 = (f32[4,768]{1,0:T(4,128)S(1)}, f32[4,768]{1,0:T(4,128)S(1)}, u32[]{:S(2)}, u32[]{:S(2)}) collective-permute-start(f32[4,768]{1,0:T(4,128)S(1)} %pad_maximum_fusion.15), channel_id=1, source_target_pairs={{0,8},{8,0},{16,24},{24,16},{1,9},{9,1},{17,25},{25,17},{2,10},{10... | collective-permute-start | bytes 36872 | tf_op jit(solution)/shard_map/ppermute | solution.py:463
  240.7 11.8 %collective-permute-start.37 = (bf16[2,96,768]{2,1,0:T(8,128)(2,1)S(1)}, bf16[2,96,768]{2,1,0:T(8,128)(2,1)S(1)}, u32[]{:S(2)}, u32[]{:S(2)}) collective-permute-start(bf16[2,96,768]{2,1,0:T(8,128)(2,1)S(1)} %add_convert_fusion.3), channel_id=1, source_target_pairs={{0,16},{8,24},{16,0},{24,8},{1,17},{9,25},{17,1},{25,9},{2,18},{10... | collective-permute-start | bytes 884744 | tf_op jit(solution)/shard_map/ppermute | solution.py:463
  243.6 12.5 %collective-permute-start.38 = (bf16[2,48,768]{2,1,0:T(8,128)(2,1)S(1)}, bf16[2,48,768]{2,1,0:T(8,128)(2,1)S(1)}, u32[]{:S(2)}, u32[]{:S(2)}) collective-permute-start(bf16[2,48,768]{2,1,0:T(8,128)(2,1)S(1)} %get-tuple-element.476), channel_id=1, source_target_pairs={{0,4},{1,5},{2,6},{3,7},{4,0},{5,1},{6,2},{7,3},{8,12},{9,13},{10,... | collective-permute-start | bytes 442376 | tf_op jit(solution)/shard_map/ppermute | solution.py:463
  246.6 9.5 %collective-permute-start.39 = (bf16[2,48,768]{2,1,0:T(8,128)(2,1)S(1)}, bf16[2,48,768]{2,1,0:T(8,128)(2,1)S(1)}, u32[]{:S(2)}, u32[]{:S(2)}) collective-permute-start(bf16[2,48,768]{2,1,0:T(8,128)(2,1)S(1)} %get-tuple-element.475), channel_id=1, source_target_pairs={{0,2},{1,3},{2,0},{3,1},{4,6},{5,7},{6,4},{7,5},{8,10},{9,11},{10,... | collective-permute-start | bytes 442376 | tf_op jit(solution)/shard_map/ppermute | solution.py:463
  247.1 10.7 %collective-permute-start.40 = (bf16[2,48,768]{2,1,0:T(8,128)(2,1)S(1)}, bf16[2,48,768]{2,1,0:T(8,128)(2,1)S(1)}, u32[]{:S(2)}, u32[]{:S(2)}) collective-permute-start(bf16[2,48,768]{2,1,0:T(8,128)(2,1)S(1)} %get-tuple-element.474), channel_id=1, source_target_pairs={{0,6},{1,7},{2,4},{3,5},{4,2},{5,3},{6,0},{7,1},{8,14},{9,15},{10,... | collective-permute-start | bytes 442376 | tf_op jit(solution)/shard_map/ppermute | solution.py:463
  248.8 3.7 %collective-permute-start.33 = (f32[4,768]{1,0:T(4,128)S(1)}, f32[4,768]{1,0:T(4,128)S(1)}, u32[]{:S(2)}, u32[]{:S(2)}) collective-permute-start(f32[4,768]{1,0:T(4,128)S(1)} %add.260), channel_id=1, source_target_pairs={{0,16},{8,24},{16,0},{24,8},{1,17},{9,25},{17,1},{25,9},{2,18},{10... | collective-permute-start | bytes 36872 | tf_op jit(solution)/shard_map/ppermute | solution.py:463
  257.8 13.0 %collective-permute-start.43 = (bf16[2,48,768]{2,1,0:T(8,128)(2,1)S(1)}, bf16[2,48,768]{2,1,0:T(8,128)(2,1)S(1)}, u32[]{:S(2)}, u32[]{:S(2)}) collective-permute-start(bf16[2,48,768]{2,1,0:T(8,128)(2,1)S(1)} %add_convert_fusion.6), channel_id=1, source_target_pairs={{0,16},{8,24},{16,0},{24,8},{1,17},{9,25},{17,1},{25,9},{2,18},{10... | collective-permute-start | bytes 442376 | tf_op jit(solution)/shard_map/ppermute | solution.py:730
  258.4 12.4 %collective-permute-start.44 = (bf16[2,48,768]{2,1,0:T(8,128)(2,1)S(1)}, bf16[2,48,768]{2,1,0:T(8,128)(2,1)S(1)}, u32[]{:S(2)}, u32[]{:S(2)}) collective-permute-start(bf16[2,48,768]{2,1,0:T(8,128)(2,1)S(1)} %add_convert_fusion.6), channel_id=1, source_target_pairs={{0,8},{8,0},{16,24},{24,16},{1,9},{9,1},{17,25},{25,17},{2,10},{10... | collective-permute-start | bytes 442376 | tf_op jit(solution)/shard_map/ppermute | solution.py:730
  258.4 12.4 %collective-permute-start.45 = (bf16[2,48,768]{2,1,0:T(8,128)(2,1)S(1)}, bf16[2,48,768]{2,1,0:T(8,128)(2,1)S(1)}, u32[]{:S(2)}, u32[]{:S(2)}) collective-permute-start(bf16[2,48,768]{2,1,0:T(8,128)(2,1)S(1)} %add_convert_fusion.6), channel_id=1, source_target_pairs={{0,24},{8,16},{16,8},{24,0},{1,25},{9,17},{17,9},{25,1},{2,26},{10... | collective-permute-start | bytes 442376 | tf_op jit(solution)/shard_map/ppermute | solution.py:730
  260.0 3.7 %collective-permute-start.36 = (f32[4,768]{1,0:T(4,128)S(1)}, f32[4,768]{1,0:T(4,128)S(1)}, u32[]{:S(2)}, u32[]{:S(2)}) collective-permute-start(f32[4,768]{1,0:T(4,128)S(1)} %add.266), channel_id=1, source_target_pairs={{0,1},{1,0},{2,3},{3,2},{4,5},{5,4},{6,7},{7,6},{8,9},{9,8},{10,11... | collective-permute-start | bytes 36872 | tf_op jit(solution)/shard_map/ppermute | solution.py:463
  263.7 3.8 %collective-permute-start.41 = (f32[4,768]{1,0:T(4,128)S(1)}, f32[4,768]{1,0:T(4,128)S(1)}, u32[]{:S(2)}, u32[]{:S(2)}) collective-permute-start(f32[4,768]{1,0:T(4,128)S(1)} %add.270), channel_id=1, source_target_pairs={{0,2},{1,3},{2,0},{3,1},{4,6},{5,7},{6,4},{7,5},{8,10},{9,11},{10,... | collective-permute-start | bytes 36872 | tf_op jit(solution)/shard_map/ppermute | solution.py:463
  266.0 7.1 %collective-permute-start.46 = (bf16[2,2,96,768]{3,2,1,0:T(8,128)(2,1)S(1)}, bf16[2,2,96,768]{3,2,1,0:T(8,128)(2,1)S(1)}, u32[]{:S(2)}, u32[]{:S(2)}) collective-permute-start(bf16[2,2,96,768]{3,2,1,0:T(8,128)(2,1)S(1)} %maximum_select_fusion.1), channel_id=1, source_target_pairs={{0,8},{8,0},{16,24},{24,16},{1,9},{9,1},{17,25},{25,17},{2,10},{10... | collective-permute-start | bytes 1769480 | tf_op jit(solution)/shard_map/ppermute | solution.py:463
  267.6 4.9 %collective-permute-start.42 = (f32[4,768]{1,0:T(4,128)S(1)}, f32[4,768]{1,0:T(4,128)S(1)}, u32[]{:S(2)}, u32[]{:S(2)}) collective-permute-start(f32[4,768]{1,0:T(4,128)S(1)} %add.271), channel_id=1, source_target_pairs={{0,4},{1,5},{2,6},{3,7},{4,0},{5,1},{6,2},{7,3},{8,12},{9,13},{10,... | collective-permute-start | bytes 36872 | tf_op jit(solution)/shard_map/ppermute | solution.py:463
  (70 other events, 336.7 us)
where the time goes:
time: 282 us; the launch traced here: 277 us
  Pallas kernels  97.3 us (35%)
  waiting for transfers between devices  62.8 us (22%)
  starting transfers between devices  41 us (15%)
  local copies, waits for them, and re-layouts  26 us (9%)
  other arithmetic  24.8 us (9%)
  matrix products  22.4 us (8%)
    ppermute x44, waiting for transfers between devices, swap(): return lax.ppermute(values, name, [(i, i ^ mask) for i in range(size)])  62.8 us
    pallas_call x2, Pallas kernels, feed_forward(): pl.pallas_call(feed_forward_kernel, grid=(hidden // part,), in_specs=[who...  42.6 us
    ppermute x44, starting transfers between devices, swap(): return lax.ppermute(values, name, [(i, i ^ mask) for i in range(size)])  38.8 us
    pallas_call x2, Pallas kernels, attend_backward(): pl.pallas_call(attend_backward_kernel, grid_spec=pltpu.PrefetchScalarGrid...  27.8 us
    dot_general x18, matrix products, dot(): lax.dot_general(left, right, (dims, ((), ())), preferred_element_type=F32)  22.4 us
    pallas_call x2, Pallas kernels, attend_forward(): pl.pallas_call(attend_forward_kernel, grid_spec=pltpu.PrefetchScalarGridS...  17.6 us
    unnamed x145, local copies, waits for them, and re-layouts  16.5 us
    convert_element_type x12, other arithmetic, add(): functools.reduce(jnp.add, [item.astype(F32) for item in terms]).astype(BF16)  7.36 us
  transfers between devices with their start and end apart: 47, of which 19 were waited for; matrix products, arithmetic and copies ran while one was open for 18% of the time, Pallas kernels for 27%

commit v1 on v0

--- a/solution.py
+++ b/solution.py
@@ -710,7 +710,7 @@
     )
     mlp_got = swap(mlp_sum, "y")
     norm_sums = line(jnp.add, norm_sums, got)
-    got = swap(norm_sums, "y")
+    got = swap(norm_sums, "x")
 
     def attn_sum_z(mine, got, from_y, from_x):
         from_x = from_x.reshape(2, -1, width)
@@ -724,28 +724,28 @@
         return order(at_core, order(at_y, piece, y), order(at_y, core, both))
 
     norm_sums = line(jnp.add, norm_sums, got)
-    got = swap(norm_sums, "x")
+    got = swap(norm_sums, "z1")
+    norm_sums = line(jnp.add, norm_sums, got)
+    got = swap(norm_sums, "z2")
     attn_sum = line(lambda _, *terms: add(*terms), mlp_got, attn_mine, *attn_z)
     attn_got = [
         lax.ppermute(attn_sum, "dp", [(i, i ^ mask) for i in range(4)]) for mask in (2, 1, 3)
     ]
-    norm_sums = line(jnp.add, norm_sums, got)
-    got = swap(norm_sums, "z1")
     mlp_sum = line(functools.partial(order, at_y), mlp_sum, mlp_got)
     mlp_got = swap(mlp_sum, "core")
     norm_sums = line(jnp.add, norm_sums, got)
-    got = swap(norm_sums, "z2")
+    got = swap(norm_sums, "y")
     attn_sum = line(in_order, attn_sum, *attn_got)
     attn_sum = line(
         lambda item: item.transpose(1, 2, 0, 3, 4).reshape(4, local, width).astype(F32), attn_sum
     )
     attn_sums = line(lambda item: (item[0].T, item[1].T, item[2].T, item[3]), attn_sum)
-    norm_sums = line(jnp.add, norm_sums, got)
     mlp_sum = line(functools.partial(order, at_core), mlp_sum, mlp_got)
     up_sum, down_sum = line(
         lambda item: tuple(item.transpose(2, 1, 0, 3, 4).reshape(2, -1, width).astype(F32)), mlp_sum
     )
     up_sum = line(jnp.transpose, up_sum)
+    norm_sums = line(jnp.add, norm_sums, got)
     norm_sums = lax.dynamic_slice_in_dim(norm_sums, at_mp * (width // 8), width // 8, 1)
     return (
         output,

time: 282 us -> 277 us (0.982)
  Pallas kernels: 97.3 us -> 91.6 us
    pallas_call x2, Pallas kernels: 27.8 us -> 24.1 us  [attend_backward(): pl.pallas_call(attend_backward_kernel, grid_spec=pltpu.PrefetchScalarGrid...]
  transfers between devices with their start and end apart: 47 -> 47, of which waited for: 19 -> 16; matrix products, arithmetic and copies ran while one was open for 18% -> 19% of each run, Pallas kernels for 27% -> 26%
where the time goes in v1:
time: 277 us; the launch traced here: 272 us
  Pallas kernels  91.6 us (33%)
  waiting for transfers between devices  61.5 us (22%)
  starting transfers between devices  43.6 us (16%)
  local copies, waits for them, and re-layouts  25.9 us (9%)
  other arithmetic  24.6 us (9%)
  matrix products  22.4 us (8%)
    ppermute x44, waiting for transfers between devices, swap(): return lax.ppermute(values, name, [(i, i ^ mask) for i in range(size)])  61.5 us
    pallas_call x2, Pallas kernels, feed_forward(): pl.pallas_call(feed_forward_kernel, grid=(hidden // part,), in_specs=[who...  42.6 us
    ppermute x44, starting transfers between devices, swap(): return lax.ppermute(values, name, [(i, i ^ mask) for i in range(size)])  41.4 us
    pallas_call x2, Pallas kernels, attend_backward(): pl.pallas_call(attend_backward_kernel, grid_spec=pltpu.PrefetchScalarGrid...  24.1 us
    dot_general x18, matrix products, dot(): lax.dot_general(left, right, (dims, ((), ())), preferred_element_type=F32)  22.4 us
    unnamed x145, local copies, waits for them, and re-layouts  16.5 us
    pallas_call x2, Pallas kernels, attend_forward(): pl.pallas_call(attend_forward_kernel, grid_spec=pltpu.PrefetchScalarGridS...  15.5 us
    convert_element_type x12, other arithmetic, add(): functools.reduce(jnp.add, [item.astype(F32) for item in terms]).astype(BF16)  7.09 us
  transfers between devices with their start and end apart: 47, of which 16 were waited for; matrix products, arithmetic and copies ran while one was open for 19% of the time, Pallas kernels for 26%

profile of v1, /device:TPU:0, one launch (start us, length us, event | category | flops | bytes accessed | tf_op | source)
XLA Modules:
  0.0 272.1 jit_solution(2155006141929493275)
XLA Ops:
  2.0 4.1 %collective-permute-start = (bf16[2,48,768]{2,1,0:T(8,128)(2,1)S(1)}, bf16[2,48,768]{2,1,0:T(8,128)(2,1)}, u32[]{:S(2)}, u32[]{:S(2)}) collective-permute-start(bf16[2,48,768]{2,1,0:T(8,128)(2,1)S(1)} %dynamic-slice_bitcast_fusion), channel_id=1, source_target_pairs={{0,4},{1,5},{2,6},{3,7},{4,0},{5,1},{6,2},{7,3},{8,12},{9,13},{10,... | collective-permute-start | bytes 442376 | tf_op jit(solution)/shard_map/ppermute | solution.py:463
  6.1 1.6 collective-permute-start.1
  11.3 1.8 fusion.5
  13.3 1.6 collective-permute-done
  15.8 2.8 %collective-permute-done.2 = bf16[2,48,768]{2,1,0:T(8,128)(2,1)} collective-permute-done((bf16[2,48,768]{2,1,0:T(8,128)(2,1)S(1)}, bf16[2,48,768]{2,1,0:T(8,128)(2,1)}, u32[]{:S(2)}, u32[]{:S(2)}) %collective-permute-start.2) | collective-permute-done | bytes 147488 | tf_op jit(solution)/shard_map/ppermute | solution.py:463
  18.6 4.3 %collective-permute-done.3 = bf16[2,96,768]{2,1,0:T(8,128)(2,1)S(1)} collective-permute-done((bf16[2,96,768]{2,1,0:T(8,128)(2,1)S(1)}, bf16[2,96,768]{2,1,0:T(8,128)(2,1)S(1)}, u32[]{:S(2)}, u32[]{:S(2)}) %collective-permute-start.3) | collective-permute-done | bytes 294944 | tf_op jit(solution)/shard_map/ppermute | solution.py:463
  24.0 1.6 collective-permute-start.4
  25.7 1.5 collective-permute-start.5
  28.5 13.4 %collective-permute-done.6 = bf16[2,96,768]{2,1,0:T(8,128)(2,1)S(1)} collective-permute-done((bf16[2,96,768]{2,1,0:T(8,128)(2,1)S(1)}, bf16[2,96,768]{2,1,0:T(8,128)(2,1)S(1)}, u32[]{:S(2)}, u32[]{:S(2)}) %collective-permute-start.6) | collective-permute-done | bytes 294944 | tf_op jit(solution)/shard_map/ppermute | solution.py:463
  43.0 2.8 %collective-permute-start.8 = (bf16[2,96,768]{2,1,0:T(8,128)(2,1)S(1)}, bf16[2,96,768]{2,1,0:T(8,128)(2,1)}, u32[]{:S(2)}, u32[]{:S(2)}) collective-permute-start(bf16[2,96,768]{2,1,0:T(8,128)(2,1)S(1)} %fusion.29), channel_id=1, source_target_pairs={{0,6},{1,7},{2,4},{3,5},{4,2},{5,3},{6,0},{7,1},{8,14},{9,15},{10,... | collective-permute-start | bytes 884744 | tf_op jit(solution)/shard_map/ppermute | solution.py:463
  48.0 2.1 copy-done.34
  50.1 1.4 convolution_convert_fusion.1
  52.4 2.1 collective-permute-done.8
  56.8 7.9 %attend_forward.2 = (bf16[2,192,1024]{2,1,0:T(8,128)(2,1)S(1)}, f32[4,8,256]{2,1,0:T(8,128)S(1)}) custom-call(s32[8]{0:T(128)S(1)} %subtract_minimum_fusion.first_ref, s32[8]{0:T(128)S(1)} %select_reduce_fusion.kind_ref, s32[1]{0:T(128)} %bitcast.2.flip_ref, s32[1,1024]{1,0:T(1,128)S(1)} %constant_dynamic-slice_fusion.2, ...), custom_call_target="tpu_custom_call" | custom-call | tf_op jit(solution)/shard_map/attend_forward/pallas_call | solution.py:256
  64.9 1.5 copy-done.4
  66.6 7.4 %collective-permute-done.10 = bf16[384,768]{1,0:T(8,128)(2,1)S(1)} collective-permute-done((bf16[384,768]{1,0:T(8,128)(2,1)S(1)}, bf16[384,768]{1,0:T(8,128)(2,1)S(1)}, u32[]{:S(2)}, u32[]{:S(2)}) %collective-permute-start.10) | collective-permute-done | bytes 589856 | tf_op jit(solution)/shard_map/ppermute | solution.py:463
  78.4 1.4 convolution_convert_fusion
  79.8 7.6 %attend_forward.3 = (bf16[2,192,1024]{2,1,0:T(8,128)(2,1)S(1)}, f32[4,8,256]{2,1,0:T(8,128)S(1)}) custom-call(s32[8]{0:T(128)S(1)} %subtract_minimum_fusion.first_ref, s32[8]{0:T(128)S(1)} %select_reduce_fusion.kind_ref, s32[1]{0:T(128)} %bitcast.2.flip_ref, s32[1,1024]{1,0:T(1,128)S(1)} %constant_dynamic-slice_fusion.2, ...), custom_call_target="tpu_custom_call" | custom-call | tf_op jit(solution)/shard_map/attend_forward/pallas_call | solution.py:256
  90.3 11.2 %collective-permute-done.15 = bf16[2,384,768]{2,1,0:T(8,128)(2,1)S(1)} collective-permute-done((bf16[2,384,768]{2,1,0:T(8,128)(2,1)S(1)}, bf16[2,384,768]{2,1,0:T(8,128)(2,1)S(1)}, u32[]{:S(2)}, u32[]{:S(2)}) %collective-permute-start.15) | collective-permute-done | bytes 1179680 | tf_op jit(solution)/shard_map/ppermute | solution.py:463
  102.5 1.4 constant_dynamic-update-slice_fusion.2.up_ref
  104.2 1.7 pad_maximum_fusion
  107.5 21.8 %feed_forward.2 = (bf16[1024,768]{1,0:T(8,128)(2,1)}, f32[1024,768]{1,0:T(8,128)}, bf16[1536,768]{1,0:T(8,128)(2,1)}, bf16[1536,768]{1,0:T(8,128)(2,1)}) custom-call(bf16[1024,768]{1,0:T(8,128)(2,1)} %copy-done.38, bf16[1024,768]{1,0:T(8,128)(2,1)} %copy-done.37, bf16[1536,768]{1,0:T(8,128)(2,1)} %copy-done.22, bf16[1536,768]{1,0:T(8,128)(2,1)} %bitcast.278), custom_call_target="tpu_custom_call" | custom-call | tf_op jit(solution)/shard_map/feed_forward/pallas_call | solution.py:360
  129.8 20.8 %feed_forward.3 = (f32[1024,768]{1,0:T(8,128)}, f32[1024,768]{1,0:T(8,128)}, bf16[1536,768]{1,0:T(8,128)(2,1)}, bf16[1536,768]{1,0:T(8,128)(2,1)}) custom-call(bf16[1024,768]{1,0:T(8,128)(2,1)} %copy-done.24, bf16[1024,768]{1,0:T(8,128)(2,1)} %cot_ref.1, bf16[1536,768]{1,0:T(8,128)(2,1)} %copy-done.22, bf16[1536,768]{1,0:T(8,128)(2,1)} %bitcast.279, ...), custom_call_target="tpu_custom_call" | custom-call | tf_op jit(solution)/shard_map/feed_forward/pallas_call | solution.py:360
  150.6 1.5 slice.285
  155.1 5.9 %middle.1 = (bf16[1024,768]{1,0:T(8,128)(2,1)}, f32[1024,768]{1,0:T(8,128)S(1)}, bf16[1024,768]{1,0:T(8,128)(2,1)S(1)}, f32[8,768]{1,0:T(8,128)S(1)}) custom-call(f32[1024,768]{1,0:T(8,128)S(1)} %get-tuple-element.291.residual_ref, bf16[1024,768]{1,0:T(8,128)(2,1)S(1)} %copy-done.5, f32[1,768]{1,0:T(1,128)S(1)} %broadcast_in_dim.18.gain_ref, ...), custom_call_target="tpu_custom_call" | custom-call | tf_op jit(solution)/shard_map/middle/pallas_call | solution.py:407
  164.5 12.1 %attend_backward.2 = (bf16[2,2,192,1024]{3,2,1,0:T(8,128)(2,1)S(1)}, bf16[2,192,1024]{2,1,0:T(8,128)(2,1)S(1)}) custom-call(s32[8]{0:T(128)S(1)} %subtract_minimum_fusion.first_ref, s32[8]{0:T(128)S(1)} %select_reduce_fusion.kind_ref, s32[1]{0:T(128)} %bitcast.2.flip_ref, s32[1,1024]{1,0:T(1,128)S(1)} %constant_dynamic-slice_fusion.2, ...), custom_call_target="tpu_custom_call" | custom-call | tf_op jit(solution)/shard_map/attend_backward/pallas_call | solution.py:284
  177.4 1.4 convolution_convert_fusion.3
  184.9 1.4 fusion.41
  186.4 2.6 convolution_add_fusion
  189.0 1.6 convolution_convert_fusion.9
  190.6 1.7 convolution_convert_fusion.4
  193.5 3.0 %collective-permute-done.22 = bf16[384,768]{1,0:T(8,128)(2,1)S(1)} collective-permute-done((bf16[384,768]{1,0:T(8,128)(2,1)S(1)}, bf16[384,768]{1,0:T(8,128)(2,1)S(1)}, u32[]{:S(2)}, u32[]{:S(2)}) %collective-permute-start.22) | collective-permute-done | bytes 589856 | tf_op jit(solution)/shard_map/ppermute | solution.py:463
  196.5 2.7 %collective-permute-done.21 = bf16[384,768]{1,0:T(8,128)(2,1)S(1)} collective-permute-done((bf16[384,768]{1,0:T(8,128)(2,1)S(1)}, bf16[384,768]{1,0:T(8,128)(2,1)S(1)}, u32[]{:S(2)}, u32[]{:S(2)}) %collective-permute-start.21) | collective-permute-done | bytes 589856 | tf_op jit(solution)/shard_map/ppermute | solution.py:463
  204.9 12.0 %attend_backward.3 = (bf16[2,2,192,1024]{3,2,1,0:T(8,128)(2,1)S(1)}, bf16[2,192,1024]{2,1,0:T(8,128)(2,1)S(1)}) custom-call(s32[8]{0:T(128)S(1)} %subtract_minimum_fusion.first_ref, s32[8]{0:T(128)S(1)} %select_reduce_fusion.kind_ref, s32[1]{0:T(128)} %bitcast.2.flip_ref, s32[1,1024]{1,0:T(1,128)S(1)} %constant_dynamic-slice_fusion.2, ...), custom_call_target="tpu_custom_call" | custom-call | tf_op jit(solution)/shard_map/attend_backward/pallas_call | solution.py:284
  220.2 1.5 collective-permute-start.32
  222.5 1.4 convolution_convert_fusion.2
  226.6 2.4 collective-permute-start.35
  229.4 1.4 fusion.42
  233.8 3.4 %last.1 = (bf16[1024,768]{1,0:T(8,128)(2,1)}, f32[8,768]{1,0:T(8,128)S(1)}) custom-call(bf16[1024,768]{1,0:T(8,128)(2,1)S(1)} %copy-done.3, f32[1024,768]{1,0:T(8,128)S(1)} %add_add_fusion.grad_ref, f32[1024,768]{1,0:T(8,128)S(1)} %copy-done.11, f32[1,768]{1,0:T(1,128)S(1)} %broadcast_in_dim.19.gain_ref), custom_call_target="tpu_custom_call" | custom-call | tf_op jit(solution)/shard_map/last/pallas_call | solution.py:436
  240.5 2.1 collective-permute-start.38
  242.6 2.0 collective-permute-done.34
  246.8 2.7 %collective-permute-start.41 = (bf16[2,48,768]{2,1,0:T(8,128)(2,1)S(1)}, bf16[2,48,768]{2,1,0:T(8,128)(2,1)S(1)}, u32[]{:S(2)}, u32[]{:S(2)}) collective-permute-start(bf16[2,48,768]{2,1,0:T(8,128)(2,1)S(1)} %get-tuple-element.474), channel_id=1, source_target_pairs={{0,6},{1,7},{2,4},{3,5},{4,2},{5,3},{6,0},{7,1},{8,14},{9,15},{10,... | collective-permute-start | bytes 442376 | tf_op jit(solution)/shard_map/ppermute | solution.py:463
  250.5 2.7 %collective-permute-done.33 = f32[4,768]{1,0:T(4,128)S(1)} collective-permute-done((f32[4,768]{1,0:T(4,128)S(1)}, f32[4,768]{1,0:T(4,128)S(1)}, u32[]{:S(2)}, u32[]{:S(2)}) %collective-permute-start.33) | collective-permute-done | bytes 12320 | tf_op jit(solution)/shard_map/ppermute | solution.py:463
  253.6 4.1 %collective-permute-done.36 = f32[4,768]{1,0:T(4,128)S(1)} collective-permute-done((f32[4,768]{1,0:T(4,128)S(1)}, f32[4,768]{1,0:T(4,128)S(1)}, u32[]{:S(2)}, u32[]{:S(2)}) %collective-permute-start.36) | collective-permute-done | bytes 12320 | tf_op jit(solution)/shard_map/ppermute | solution.py:463
  260.1 3.2 %collective-permute-start.37 = (f32[4,768]{1,0:T(4,128)S(1)}, f32[4,768]{1,0:T(4,128)S(1)}, u32[]{:S(2)}, u32[]{:S(2)}) collective-permute-start(f32[4,768]{1,0:T(4,128)S(1)} %add.267), channel_id=1, source_target_pairs={{0,4},{1,5},{2,6},{3,7},{4,0},{5,1},{6,2},{7,3},{8,12},{9,13},{10,... | collective-permute-start | bytes 36872 | tf_op jit(solution)/shard_map/ppermute | solution.py:463
  263.4 1.5 collective-permute-done.37
  264.9 1.6 collective-permute-start.42
  269.7 1.4 copy.56
  (317 shorter events, 68.4 us)
Async XLA Ops:
  2.0 12.9 %collective-permute-start = (bf16[2,48,768]{2,1,0:T(8,128)(2,1)S(1)}, bf16[2,48,768]{2,1,0:T(8,128)(2,1)}, u32[]{:S(2)}, u32[]{:S(2)}) collective-permute-start(bf16[2,48,768]{2,1,0:T(8,128)(2,1)S(1)} %dynamic-slice_bitcast_fusion), channel_id=1, source_target_pairs={{0,4},{1,5},{2,6},{3,7},{4,0},{5,1},{6,2},{7,3},{8,12},{9,13},{10,... | collective-permute-start | bytes 442376 | tf_op jit(solution)/shard_map/ppermute | solution.py:463
  6.1 9.7 %collective-permute-start.1 = (bf16[2,48,768]{2,1,0:T(8,128)(2,1)S(1)}, bf16[2,48,768]{2,1,0:T(8,128)(2,1)}, u32[]{:S(2)}, u32[]{:S(2)}) collective-permute-start(bf16[2,48,768]{2,1,0:T(8,128)(2,1)S(1)} %dynamic-slice_bitcast_fusion), channel_id=1, source_target_pairs={{0,2},{1,3},{2,0},{3,1},{4,6},{5,7},{6,4},{7,5},{8,10},{9,11},{10,... | collective-permute-start | bytes 442376 | tf_op jit(solution)/shard_map/ppermute | solution.py:463
  7.7 10.9 %collective-permute-start.2 = (bf16[2,48,768]{2,1,0:T(8,128)(2,1)S(1)}, bf16[2,48,768]{2,1,0:T(8,128)(2,1)}, u32[]{:S(2)}, u32[]{:S(2)}) collective-permute-start(bf16[2,48,768]{2,1,0:T(8,128)(2,1)S(1)} %dynamic-slice_bitcast_fusion), channel_id=1, source_target_pairs={{0,6},{1,7},{2,4},{3,5},{4,2},{5,3},{6,0},{7,1},{8,14},{9,15},{10,... | collective-permute-start | bytes 442376 | tf_op jit(solution)/shard_map/ppermute | solution.py:463
  8.9 14.0 %collective-permute-start.3 = (bf16[2,96,768]{2,1,0:T(8,128)(2,1)S(1)}, bf16[2,96,768]{2,1,0:T(8,128)(2,1)S(1)}, u32[]{:S(2)}, u32[]{:S(2)}) collective-permute-start(bf16[2,96,768]{2,1,0:T(8,128)(2,1)S(1)} %fusion.29), channel_id=1, source_target_pairs={{0,2},{1,3},{2,0},{3,1},{4,6},{5,7},{6,4},{7,5},{8,10},{9,11},{10,... | collective-permute-start | bytes 884744 | tf_op jit(solution)/shard_map/ppermute | solution.py:463
  24.0 17.9 %collective-permute-start.4 = (bf16[4,2,48,768]{3,2,0,1:T(8,128)(2,1)S(1)}, bf16[4,2,48,768]{3,2,0,1:T(8,128)(2,1)S(1)}, u32[]{:S(2)}, u32[]{:S(2)}) collective-permute-start(bf16[4,2,48,768]{3,2,0,1:T(8,128)(2,1)S(1)} %pad_maximum_fusion.8), channel_id=1, source_target_pairs={{0,16},{8,24},{16,0},{24,8},{1,17},{9,25},{17,1},{25,9},{2,18},{10... | collective-permute-start | bytes 1769480 | tf_op jit(solution)/shard_map/ppermute | solution.py:463
  25.7 16.2 %collective-permute-start.5 = (bf16[4,2,48,768]{3,2,0,1:T(8,128)(2,1)S(1)}, bf16[4,2,48,768]{3,2,0,1:T(8,128)(2,1)S(1)}, u32[]{:S(2)}, u32[]{:S(2)}) collective-permute-start(bf16[4,2,48,768]{3,2,0,1:T(8,128)(2,1)S(1)} %pad_maximum_fusion.8), channel_id=1, source_target_pairs={{0,1},{1,0},{2,3},{3,2},{4,5},{5,4},{6,7},{7,6},{8,9},{9,8},{10,11... | collective-permute-start | bytes 1769480 | tf_op jit(solution)/shard_map/ppermute | solution.py:463
  27.2 14.7 %collective-permute-start.6 = (bf16[2,96,768]{2,1,0:T(8,128)(2,1)S(1)}, bf16[2,96,768]{2,1,0:T(8,128)(2,1)S(1)}, u32[]{:S(2)}, u32[]{:S(2)}) collective-permute-start(bf16[2,96,768]{2,1,0:T(8,128)(2,1)S(1)} %fusion.29), channel_id=1, source_target_pairs={{0,4},{1,5},{2,6},{3,7},{4,0},{5,1},{6,2},{7,3},{8,12},{9,13},{10,... | collective-permute-start | bytes 884744 | tf_op jit(solution)/shard_map/ppermute | solution.py:463
  42.9 3.4 %collective-permute-start.7 = (bf16[2,4,2,48,768]{4,3,1,0,2:T(8,128)(2,1)S(1)}, bf16[2,4,2,48,768]{4,3,1,0,2:T(8,128)(2,1)}, u32[]{:S(2)}, u32[]{:S(2)}) collective-permute-start(bf16[2,4,2,48,768]{4,3,1,0,2:T(8,128)(2,1)S(1)} %pad_maximum_fusion.1), channel_id=1, source_target_pairs={{0,8},{8,0},{16,24},{24,16},{1,9},{9,1},{17,25},{25,17},{2,10},{10... | collective-permute-start | bytes 3538952 | tf_op jit(solution)/shard_map/ppermute | solution.py:463
  43.0 11.4 %collective-permute-start.8 = (bf16[2,96,768]{2,1,0:T(8,128)(2,1)S(1)}, bf16[2,96,768]{2,1,0:T(8,128)(2,1)}, u32[]{:S(2)}, u32[]{:S(2)}) collective-permute-start(bf16[2,96,768]{2,1,0:T(8,128)(2,1)S(1)} %fusion.29), channel_id=1, source_target_pairs={{0,6},{1,7},{2,4},{3,5},{4,2},{5,3},{6,0},{7,1},{8,14},{9,15},{10,... | collective-permute-start | bytes 884744 | tf_op jit(solution)/shard_map/ppermute | solution.py:463
  45.8 18.9 %collective-permute-start.11 = (bf16[4,2,48,768]{3,2,0,1:T(8,128)(2,1)}, bf16[4,2,48,768]{3,2,0,1:T(8,128)(2,1)S(1)}, u32[]{:S(2)}, u32[]{:S(2)}) collective-permute-start(bf16[4,2,48,768]{3,2,0,1:T(8,128)(2,1)} %copy-done.62), channel_id=1, source_target_pairs={{0,16},{8,24},{16,0},{24,8},{1,17},{9,25},{17,1},{25,9},{2,18},{10... | collective-permute-start | bytes 1769480 | tf_op jit(solution)/shard_map/ppermute | solution.py:463
  55.6 18.4 %collective-permute-start.10 = (bf16[384,768]{1,0:T(8,128)(2,1)S(1)}, bf16[384,768]{1,0:T(8,128)(2,1)S(1)}, u32[]{:S(2)}, u32[]{:S(2)}) collective-permute-start(bf16[384,768]{1,0:T(8,128)(2,1)S(1)} %pad_maximum_fusion.10), channel_id=1, source_target_pairs={{0,16},{8,24},{16,0},{24,8},{1,17},{9,25},{17,1},{25,9},{2,18},{10... | collective-permute-start | bytes 1769480 | tf_op jit(solution)/shard_map/ppermute | solution.py:463
  56.2 17.8 %collective-permute-start.9 = (bf16[384,768]{1,0:T(8,128)(2,1)S(1)}, bf16[384,768]{1,0:T(8,128)(2,1)S(1)}, u32[]{:S(2)}, u32[]{:S(2)}) collective-permute-start(bf16[384,768]{1,0:T(8,128)(2,1)S(1)} %pad_maximum_fusion.9), channel_id=1, source_target_pairs={{0,1},{1,0},{2,3},{3,2},{4,5},{5,4},{6,7},{7,6},{8,9},{9,8},{10,11... | collective-permute-start | bytes 1769480 | tf_op jit(solution)/shard_map/ppermute | solution.py:463
  64.9 11.6 %collective-permute-start.12 = (bf16[2,4,2,48,768]{4,3,1,0,2:T(8,128)(2,1)S(1)}, bf16[2,4,2,48,768]{4,3,1,0,2:T(8,128)(2,1)S(1)}, u32[]{:S(2)}, u32[]{:S(2)}) collective-permute-start(bf16[2,4,2,48,768]{4,3,1,0,2:T(8,128)(2,1)S(1)} %pad_maximum_fusion.3), channel_id=1, source_target_pairs={{0,8},{8,0},{16,24},{24,16},{1,9},{9,1},{17,25},{25,17},{2,10},{10... | collective-permute-start | bytes 3538952 | tf_op jit(solution)/shard_map/ppermute | solution.py:463
  66.4 21.0 %collective-permute-start.13 = (bf16[1024,768]{1,0:T(8,128)(2,1)S(1)}, bf16[1024,768]{1,0:T(8,128)(2,1)S(1)}, u32[]{:S(2)}, u32[]{:S(2)}) collective-permute-start(bf16[1024,768]{1,0:T(8,128)(2,1)S(1)} %copy-done.4), channel_id=1, source_target_pairs={{0,8},{8,0},{16,24},{24,16},{1,9},{9,1},{17,25},{25,17},{2,10},{10... | collective-permute-start | bytes 4718600 | tf_op jit(solution)/shard_map/ppermute | solution.py:463
  74.2 27.3 %collective-permute-start.15 = (bf16[2,384,768]{2,1,0:T(8,128)(2,1)S(1)}, bf16[2,384,768]{2,1,0:T(8,128)(2,1)S(1)}, u32[]{:S(2)}, u32[]{:S(2)}) collective-permute-start(bf16[2,384,768]{2,1,0:T(8,128)(2,1)S(1)} %pad_maximum_fusion.4), channel_id=1, source_target_pairs={{0,1},{1,0},{2,3},{3,2},{4,5},{5,4},{6,7},{7,6},{8,9},{9,8},{10,11... | collective-permute-start | bytes 3538952 | tf_op jit(solution)/shard_map/ppermute | solution.py:463
  74.9 27.6 %collective-permute-start.14 = (bf16[768,768]{1,0:T(8,128)(2,1)S(1)}, bf16[768,768]{1,0:T(8,128)(2,1)}, u32[]{:S(2)}, u32[]{:S(2)}) collective-permute-start(bf16[768,768]{1,0:T(8,128)(2,1)S(1)} %constant_dynamic-update-slice_fusion), channel_id=1, source_target_pairs={{0,16},{8,24},{16,0},{24,8},{1,17},{9,25},{17,1},{25,9},{2,18},{10... | collective-permute-start | bytes 3538952 | tf_op jit(solution)/shard_map/ppermute | solution.py:463
  90.2 16.2 %collective-permute-start.16 = (bf16[1024,768]{1,0:T(8,128)(2,1)S(1)}, bf16[1024,768]{1,0:T(8,128)(2,1)S(1)}, u32[]{:S(2)}, u32[]{:S(2)}) collective-permute-start(bf16[1024,768]{1,0:T(8,128)(2,1)S(1)} %add_convert_fusion.norm_ref), channel_id=1, source_target_pairs={{0,8},{8,0},{16,24},{24,16},{1,9},{9,1},{17,25},{25,17},{2,10},{10... | collective-permute-start | bytes 4718600 | tf_op jit(solution)/shard_map/ppermute | solution.py:463
  129.3 25.1 %collective-permute-start.18 = (f32[1024,768]{1,0:T(8,128)}, f32[1024,768]{1,0:T(8,128)}, u32[]{:S(2)}, u32[]{:S(2)}) collective-permute-start(f32[1024,768]{1,0:T(8,128)} %get-tuple-element.278), channel_id=1, source_target_pairs={{0,8},{8,0},{16,24},{24,16},{1,9},{9,1},{17,25},{25,17},{2,10},{10... | collective-permute-start | bytes 9437192 | tf_op jit(solution)/shard_map/ppermute | solution.py:463
  129.3 25.1 %collective-permute-start.17 = (bf16[1024,768]{1,0:T(8,128)(2,1)}, bf16[1024,768]{1,0:T(8,128)(2,1)}, u32[]{:S(2)}, u32[]{:S(2)}) collective-permute-start(bf16[1024,768]{1,0:T(8,128)(2,1)} %get-tuple-element.277), channel_id=1, source_target_pairs={{0,8},{8,0},{16,24},{24,16},{1,9},{9,1},{17,25},{25,17},{2,10},{10... | collective-permute-start | bytes 4718600 | tf_op jit(solution)/shard_map/ppermute | solution.py:463
  152.9 28.0 %collective-permute-start.20 = (bf16[2,384,768]{2,1,0:T(8,128)(2,1)S(1)}, bf16[2,384,768]{2,1,0:T(8,128)(2,1)S(1)}, u32[]{:S(2)}, u32[]{:S(2)}) collective-permute-start(bf16[2,384,768]{2,1,0:T(8,128)(2,1)S(1)} %pad_maximum_fusion.6), channel_id=1, source_target_pairs={{0,1},{1,0},{2,3},{3,2},{4,5},{5,4},{6,7},{7,6},{8,9},{9,8},{10,11... | collective-permute-start | bytes 3538952 | tf_op jit(solution)/shard_map/ppermute | solution.py:463
  153.9 27.7 %collective-permute-start.19 = (bf16[768,768]{1,0:T(8,128)(2,1)S(1)}, bf16[768,768]{1,0:T(8,128)(2,1)S(1)}, u32[]{:S(2)}, u32[]{:S(2)}) collective-permute-start(bf16[768,768]{1,0:T(8,128)(2,1)S(1)} %slice.285), channel_id=1, source_target_pairs={{0,16},{8,24},{16,0},{24,8},{1,17},{9,25},{17,1},{25,9},{2,18},{10... | collective-permute-start | bytes 3538952 | tf_op jit(solution)/shard_map/ppermute | solution.py:463
  162.7 29.8 %copy-start.40 = (bf16[384,768]{1,0:T(8,128)(2,1)}, bf16[384,768]{1,0:T(8,128)(2,1)S(1)}, u32[]{:S(2)}) copy-start(bf16[384,768]{1,0:T(8,128)(2,1)S(1)} %convolution_convert_fusion.11) | copy-start | bytes 1769476
  178.9 13.4 %collective-permute-start.23 = (bf16[2,192,768]{2,1,0:T(8,128)(2,1)S(1)}, bf16[2,192,768]{2,1,0:T(8,128)(2,1)S(1)}, u32[]{:S(2)}, u32[]{:S(2)}) collective-permute-start(bf16[2,192,768]{2,1,0:T(8,128)(2,1)S(1)} %bitcast.322), channel_id=1, source_target_pairs={{0,8},{8,0},{16,24},{24,16},{1,9},{9,1},{17,25},{25,17},{2,10},{10... | collective-permute-start | bytes 1769480 | tf_op jit(solution)/shard_map/ppermute | solution.py:463
  179.4 12.9 %collective-permute-start.24 = (bf16[192,768]{1,0:T(8,128)(2,1)S(1)}, bf16[192,768]{1,0:T(8,128)(2,1)S(1)}, u32[]{:S(2)}, u32[]{:S(2)}) collective-permute-start(bf16[192,768]{1,0:T(8,128)(2,1)S(1)} %slice.357), channel_id=1, source_target_pairs={{0,8},{8,0},{16,24},{24,16},{1,9},{9,1},{17,25},{25,17},{2,10},{10... | collective-permute-start | bytes 884744 | tf_op jit(solution)/shard_map/ppermute | solution.py:463
  179.5 12.8 %collective-permute-start.25 = (bf16[192,768]{1,0:T(8,128)(2,1)S(1)}, bf16[192,768]{1,0:T(8,128)(2,1)S(1)}, u32[]{:S(2)}, u32[]{:S(2)}) collective-permute-start(bf16[192,768]{1,0:T(8,128)(2,1)S(1)} %slice.290), channel_id=1, source_target_pairs={{0,8},{8,0},{16,24},{24,16},{1,9},{9,1},{17,25},{25,17},{2,10},{10... | collective-permute-start | bytes 884744 | tf_op jit(solution)/shard_map/ppermute | solution.py:463
  181.7 14.8 %collective-permute-start.22 = (bf16[384,768]{1,0:T(8,128)(2,1)S(1)}, bf16[384,768]{1,0:T(8,128)(2,1)S(1)}, u32[]{:S(2)}, u32[]{:S(2)}) collective-permute-start(bf16[384,768]{1,0:T(8,128)(2,1)S(1)} %fusion.6), channel_id=1, source_target_pairs={{0,16},{8,24},{16,0},{24,8},{1,17},{9,25},{17,1},{25,9},{2,18},{10... | collective-permute-start | bytes 1769480 | tf_op jit(solution)/shard_map/ppermute | solution.py:463
  183.8 15.5 %collective-permute-start.21 = (bf16[384,768]{1,0:T(8,128)(2,1)S(1)}, bf16[384,768]{1,0:T(8,128)(2,1)S(1)}, u32[]{:S(2)}, u32[]{:S(2)}) collective-permute-start(bf16[384,768]{1,0:T(8,128)(2,1)S(1)} %add_convert_fusion.2), channel_id=1, source_target_pairs={{0,1},{1,0},{2,3},{3,2},{4,5},{5,4},{6,7},{7,6},{8,9},{9,8},{10,11... | collective-permute-start | bytes 1769480 | tf_op jit(solution)/shard_map/ppermute | solution.py:463
  201.6 15.3 %collective-permute-start.26 = (bf16[2,192,768]{2,1,0:T(8,128)(2,1)}, bf16[2,192,768]{2,1,0:T(8,128)(2,1)}, u32[]{:S(2)}, u32[]{:S(2)}) collective-permute-start(bf16[2,192,768]{2,1,0:T(8,128)(2,1)} %pad_maximum_fusion.12), channel_id=1, source_target_pairs={{0,2},{1,3},{2,0},{3,1},{4,6},{5,7},{6,4},{7,5},{8,10},{9,11},{10,... | collective-permute-start | bytes 1769480 | tf_op jit(solution)/shard_map/ppermute | solution.py:463
  202.5 22.2 %collective-permute-start.30 = (bf16[2,192,768]{2,1,0:T(8,128)(2,1)}, bf16[2,192,768]{2,1,0:T(8,128)(2,1)S(1)}, u32[]{:S(2)}, u32[]{:S(2)}) collective-permute-start(bf16[2,192,768]{2,1,0:T(8,128)(2,1)} %pad_maximum_fusion.11), channel_id=1, source_target_pairs={{0,16},{8,24},{16,0},{24,8},{1,17},{9,25},{17,1},{25,9},{2,18},{10... | collective-permute-start | bytes 1769480 | tf_op jit(solution)/shard_map/ppermute | solution.py:463
  220.2 17.1 %collective-permute-start.32 = (bf16[2,96,768]{2,1,0:T(8,128)(2,1)S(1)}, bf16[2,96,768]{2,1,0:T(8,128)(2,1)S(1)}, u32[]{:S(2)}, u32[]{:S(2)}) collective-permute-start(bf16[2,96,768]{2,1,0:T(8,128)(2,1)S(1)} %add_convert_fusion.4), channel_id=1, source_target_pairs={{0,4},{1,5},{2,6},{3,7},{4,0},{5,1},{6,2},{7,3},{8,12},{9,13},{10,... | collective-permute-start | bytes 884744 | tf_op jit(solution)/shard_map/ppermute | solution.py:463
  224.0 5.0 %collective-permute-start.27 = (bf16[2,192,768]{2,1,0:T(8,128)(2,1)S(1)}, bf16[2,192,768]{2,1,0:T(8,128)(2,1)S(1)}, u32[]{:S(2)}, u32[]{:S(2)}) collective-permute-start(bf16[2,192,768]{2,1,0:T(8,128)(2,1)S(1)} %bitcast.323), channel_id=1, source_target_pairs={{0,8},{8,0},{16,24},{24,16},{1,9},{9,1},{17,25},{25,17},{2,10},{10... | collective-permute-start | bytes 1769480 | tf_op jit(solution)/shard_map/ppermute | solution.py:463
  224.1 4.9 %collective-permute-start.28 = (bf16[192,768]{1,0:T(8,128)(2,1)S(1)}, bf16[192,768]{1,0:T(8,128)(2,1)S(1)}, u32[]{:S(2)}, u32[]{:S(2)}) collective-permute-start(bf16[192,768]{1,0:T(8,128)(2,1)S(1)} %slice.364), channel_id=1, source_target_pairs={{0,8},{8,0},{16,24},{24,16},{1,9},{9,1},{17,25},{25,17},{2,10},{10... | collective-permute-start | bytes 884744 | tf_op jit(solution)/shard_map/ppermute | solution.py:463
  224.6 4.4 %collective-permute-start.29 = (bf16[192,768]{1,0:T(8,128)(2,1)S(1)}, bf16[192,768]{1,0:T(8,128)(2,1)S(1)}, u32[]{:S(2)}, u32[]{:S(2)}) collective-permute-start(bf16[192,768]{1,0:T(8,128)(2,1)S(1)} %slice.314), channel_id=1, source_target_pairs={{0,8},{8,0},{16,24},{24,16},{1,9},{9,1},{17,25},{25,17},{2,10},{10... | collective-permute-start | bytes 884744 | tf_op jit(solution)/shard_map/ppermute | solution.py:463
  226.6 16.0 %collective-permute-start.35 = (bf16[2,192,768]{2,1,0:T(8,128)(2,1)S(1)}, bf16[2,192,768]{2,1,0:T(8,128)(2,1)S(1)}, u32[]{:S(2)}, u32[]{:S(2)}) collective-permute-start(bf16[2,192,768]{2,1,0:T(8,128)(2,1)S(1)} %pad_maximum_fusion.13), channel_id=1, source_target_pairs={{0,1},{1,0},{2,3},{3,2},{4,5},{5,4},{6,7},{7,6},{8,9},{9,8},{10,11... | collective-permute-start | bytes 1769480 | tf_op jit(solution)/shard_map/ppermute | solution.py:463
  229.3 15.2 %collective-permute-start.34 = (bf16[2,192,768]{2,1,0:T(8,128)(2,1)S(1)}, bf16[2,192,768]{2,1,0:T(8,128)(2,1)S(1)}, u32[]{:S(2)}, u32[]{:S(2)}) collective-permute-start(bf16[2,192,768]{2,1,0:T(8,128)(2,1)S(1)} %pad_maximum_fusion.14), channel_id=1, source_target_pairs={{0,16},{8,24},{16,0},{24,8},{1,17},{9,25},{17,1},{25,9},{2,18},{10... | collective-permute-start | bytes 1769480 | tf_op jit(solution)/shard_map/ppermute | solution.py:463
  237.2 5.3 %collective-permute-start.31 = (f32[4,768]{1,0:T(4,128)S(1)}, f32[4,768]{1,0:T(4,128)S(1)}, u32[]{:S(2)}, u32[]{:S(2)}) collective-permute-start(f32[4,768]{1,0:T(4,128)S(1)} %pad_maximum_fusion.15), channel_id=1, source_target_pairs={{0,8},{8,0},{16,24},{24,16},{1,9},{9,1},{17,25},{25,17},{2,10},{10... | collective-permute-start | bytes 36872 | tf_op jit(solution)/shard_map/ppermute | solution.py:463
  240.5 17.3 %collective-permute-start.38 = (bf16[2,96,768]{2,1,0:T(8,128)(2,1)S(1)}, bf16[2,96,768]{2,1,0:T(8,128)(2,1)S(1)}, u32[]{:S(2)}, u32[]{:S(2)}) collective-permute-start(bf16[2,96,768]{2,1,0:T(8,128)(2,1)S(1)} %add_convert_fusion.3), channel_id=1, source_target_pairs={{0,16},{8,24},{16,0},{24,8},{1,17},{9,25},{17,1},{25,9},{2,18},{10... | collective-permute-start | bytes 884744 | tf_op jit(solution)/shard_map/ppermute | solution.py:463
  245.1 12.7 %collective-permute-start.39 = (bf16[2,48,768]{2,1,0:T(8,128)(2,1)S(1)}, bf16[2,48,768]{2,1,0:T(8,128)(2,1)S(1)}, u32[]{:S(2)}, u32[]{:S(2)}) collective-permute-start(bf16[2,48,768]{2,1,0:T(8,128)(2,1)S(1)} %get-tuple-element.476), channel_id=1, source_target_pairs={{0,4},{1,5},{2,6},{3,7},{4,0},{5,1},{6,2},{7,3},{8,12},{9,13},{10,... | collective-permute-start | bytes 442376 | tf_op jit(solution)/shard_map/ppermute | solution.py:463
  246.1 11.6 %collective-permute-start.40 = (bf16[2,48,768]{2,1,0:T(8,128)(2,1)S(1)}, bf16[2,48,768]{2,1,0:T(8,128)(2,1)S(1)}, u32[]{:S(2)}, u32[]{:S(2)}) collective-permute-start(bf16[2,48,768]{2,1,0:T(8,128)(2,1)S(1)} %get-tuple-element.475), channel_id=1, source_target_pairs={{0,2},{1,3},{2,0},{3,1},{4,6},{5,7},{6,4},{7,5},{8,10},{9,11},{10,... | collective-permute-start | bytes 442376 | tf_op jit(solution)/shard_map/ppermute | solution.py:463
  246.8 10.9 %collective-permute-start.41 = (bf16[2,48,768]{2,1,0:T(8,128)(2,1)S(1)}, bf16[2,48,768]{2,1,0:T(8,128)(2,1)S(1)}, u32[]{:S(2)}, u32[]{:S(2)}) collective-permute-start(bf16[2,48,768]{2,1,0:T(8,128)(2,1)S(1)} %get-tuple-element.474), channel_id=1, source_target_pairs={{0,6},{1,7},{2,4},{3,5},{4,2},{5,3},{6,0},{7,1},{8,14},{9,15},{10,... | collective-permute-start | bytes 442376 | tf_op jit(solution)/shard_map/ppermute | solution.py:463
  249.6 3.7 %collective-permute-start.33 = (f32[4,768]{1,0:T(4,128)S(1)}, f32[4,768]{1,0:T(4,128)S(1)}, u32[]{:S(2)}, u32[]{:S(2)}) collective-permute-start(f32[4,768]{1,0:T(4,128)S(1)} %add.260), channel_id=1, source_target_pairs={{0,1},{1,0},{2,3},{3,2},{4,5},{5,4},{6,7},{7,6},{8,9},{9,8},{10,11... | collective-permute-start | bytes 36872 | tf_op jit(solution)/shard_map/ppermute | solution.py:463
  253.3 4.5 %collective-permute-start.36 = (f32[4,768]{1,0:T(4,128)S(1)}, f32[4,768]{1,0:T(4,128)S(1)}, u32[]{:S(2)}, u32[]{:S(2)}) collective-permute-start(f32[4,768]{1,0:T(4,128)S(1)} %add.266), channel_id=1, source_target_pairs={{0,2},{1,3},{2,0},{3,1},{4,6},{5,7},{6,4},{7,5},{8,10},{9,11},{10,... | collective-permute-start | bytes 36872 | tf_op jit(solution)/shard_map/ppermute | solution.py:463
  257.9 8.6 %collective-permute-start.44 = (bf16[2,48,768]{2,1,0:T(8,128)(2,1)S(1)}, bf16[2,48,768]{2,1,0:T(8,128)(2,1)S(1)}, u32[]{:S(2)}, u32[]{:S(2)}) collective-permute-start(bf16[2,48,768]{2,1,0:T(8,128)(2,1)S(1)} %add_convert_fusion.6), channel_id=1, source_target_pairs={{0,16},{8,24},{16,0},{24,8},{1,17},{9,25},{17,1},{25,9},{2,18},{10... | collective-permute-start | bytes 442376 | tf_op jit(solution)/shard_map/ppermute | solution.py:732
  258.8 7.7 %collective-permute-start.45 = (bf16[2,48,768]{2,1,0:T(8,128)(2,1)S(1)}, bf16[2,48,768]{2,1,0:T(8,128)(2,1)S(1)}, u32[]{:S(2)}, u32[]{:S(2)}) collective-permute-start(bf16[2,48,768]{2,1,0:T(8,128)(2,1)S(1)} %add_convert_fusion.6), channel_id=1, source_target_pairs={{0,8},{8,0},{16,24},{24,16},{1,9},{9,1},{17,25},{25,17},{2,10},{10... | collective-permute-start | bytes 442376 | tf_op jit(solution)/shard_map/ppermute | solution.py:732
  258.8 7.7 %collective-permute-start.46 = (bf16[2,48,768]{2,1,0:T(8,128)(2,1)S(1)}, bf16[2,48,768]{2,1,0:T(8,128)(2,1)S(1)}, u32[]{:S(2)}, u32[]{:S(2)}) collective-permute-start(bf16[2,48,768]{2,1,0:T(8,128)(2,1)S(1)} %add_convert_fusion.6), channel_id=1, source_target_pairs={{0,24},{8,16},{16,8},{24,0},{1,25},{9,17},{17,9},{25,1},{2,26},{10... | collective-permute-start | bytes 442376 | tf_op jit(solution)/shard_map/ppermute | solution.py:732
  260.1 4.9 %collective-permute-start.37 = (f32[4,768]{1,0:T(4,128)S(1)}, f32[4,768]{1,0:T(4,128)S(1)}, u32[]{:S(2)}, u32[]{:S(2)}) collective-permute-start(f32[4,768]{1,0:T(4,128)S(1)} %add.267), channel_id=1, source_target_pairs={{0,4},{1,5},{2,6},{3,7},{4,0},{5,1},{6,2},{7,3},{8,12},{9,13},{10,... | collective-permute-start | bytes 36872 | tf_op jit(solution)/shard_map/ppermute | solution.py:463
  263.4 4.6 %collective-permute-start.43 = (bf16[2,2,96,768]{3,2,1,0:T(8,128)(2,1)S(1)}, bf16[2,2,96,768]{3,2,1,0:T(8,128)(2,1)S(1)}, u32[]{:S(2)}, u32[]{:S(2)}) collective-permute-start(bf16[2,2,96,768]{3,2,1,0:T(8,128)(2,1)S(1)} %maximum_select_fusion.1), channel_id=1, source_target_pairs={{0,8},{8,0},{16,24},{24,16},{1,9},{9,1},{17,25},{25,17},{2,10},{10... | collective-permute-start | bytes 1769480 | tf_op jit(solution)/shard_map/ppermute | solution.py:463
  264.9 6.1 %collective-permute-start.42 = (f32[4,768]{1,0:T(4,128)S(1)}, f32[4,768]{1,0:T(4,128)S(1)}, u32[]{:S(2)}, u32[]{:S(2)}) collective-permute-start(f32[4,768]{1,0:T(4,128)S(1)} %add.271), channel_id=1, source_target_pairs={{0,16},{8,24},{16,0},{24,8},{1,17},{9,25},{17,1},{25,9},{2,18},{10... | collective-permute-start | bytes 36872 | tf_op jit(solution)/shard_map/ppermute | solution.py:463
  (70 other events, 336.4 us)
